TPU v7x, 32 devices: a whole 2x2x4 slice. The times are simulated.
32 devices in a mesh: rows: 8 (over z, x), blk: 4 (over y, core).
Axes of the slice: x: 2, y: 2, z: 4, core: 2. Of those that a mesh axis runs over, the one named last changes fastest.
Arguments:
- inputs: bfloat16 [32, 1152, 768], P('rows', 'blk'), may hold values from -6 to 6
- image_index: int32 [32, 1152], P('rows', 'blk'), may hold values from -1 to 3, as said below
- keep_mask: int32 [32, 2], P('rows'), may hold values 0 or 1
- first_gain: float32 [768], replicated, may hold values from 0.5 to 1.5
- first_shift: float32 [768], replicated, may hold values from -2.5 to 2.5
- input_weight: bfloat16 [768, 2304], replicated, may hold values from -0.21875 to 0.21875
- input_bias: float32 [2, 768], replicated, may hold values from -2.5 to 2.5
- output_weight: bfloat16 [768, 768], replicated, may hold values from -3.5 to 3.5
- output_bias: float32 [768], replicated, may hold values from -2.5 to 2.5
- second_gain: float32 [768], replicated, may hold values from 0.5 to 1.5
- second_shift: float32 [768], replicated, may hold values from -2.5 to 2.5
- up_weight: bfloat16 [768, 3072], replicated, may hold values from -0.21875 to 0.21875
- up_bias: float32 [3072], replicated, may hold values from -2.5 to 2.5
- down_weight: bfloat16 [3072, 768], replicated, may hold values from -0.109375 to 0.109375
- down_bias: float32 [768], replicated, may hold values from -2.5 to 2.5
- cotangent: bfloat16 [32, 1152, 768], P('rows', 'blk'), may hold values from -6 to 6
Outputs:
- result: bfloat16 [32, 1152, 768], P('rows', 'blk')
- inputs_gradient: bfloat16 [32, 1152, 768], P('rows', 'blk')
- first_gain_gradient: float32 [768], replicated
- first_shift_gradient: float32 [768], replicated
- input_weight_gradient: float32 [768, 2304], replicated
- input_bias_gradient: float32 [2, 768], replicated
- output_weight_gradient: float32 [768, 768], replicated
- output_bias_gradient: float32 [768], replicated
- second_gain_gradient: float32 [768], replicated
- second_shift_gradient: float32 [768], replicated
- up_weight_gradient: float32 [768, 3072], replicated
- up_bias_gradient: float32 [3072], replicated
- down_weight_gradient: float32 [3072, 768], replicated
- down_bias_gradient: float32 [768], replicated
Inputs may be any that keep to these rules, and one draw needn't show every extreme that they name: `image_index`: in each row, images 0 to 3 each hold 194 to 282 slots, the rest of the row is padding (-1); every image and the padding of every row have slots on every device of blk.
All inputs are finite; a program needn't handle non-finite values. No bound on the sum of `keep_mask` on one device may be relied on, other than what follows from the above.
Results may differ from a plain program's by a relative error of at most 0.015.
Values may be sent and summed in bfloat16 or wider, within the bound.
No kernel may reach another device: no remote copies, remote signals or barrier semaphores. Data moves between devices by JAX's collectives and lax.ppermute only.
A program may use at most 448 MiB of HBM per device.

v0:
```python
import jax
import jax.numpy as jnp
from jax import lax
from jax.sharding import PartitionSpec as P

HEADS = 12
HEAD_DIM = 64
MICRO = 2


eps_norm = 1e-06
keep_rate = 0.9


def from_behind(value, axis, steps):
    count = lax.axis_size(axis)
    pairs = [(source, (source + steps) % count) for source in range(count)]
    return lax.ppermute(value, axis, pairs)


def norm_rows(values, gain, shift):
    centre = values - jnp.mean(values, axis=-1, keepdims=True)
    spread = jnp.mean(centre * centre, axis=-1, keepdims=True)
    return centre * lax.rsqrt(spread + eps_norm) * gain + shift


def gelu_exact(values):
    return jax.nn.gelu(values, approximate=False)


def split_heads(block):
    return block.reshape(block.shape[0], block.shape[1], HEADS, HEAD_DIM)


def take_rows(array, first_row, count_rows):
    return lax.slice_in_dim(array, first_row, first_row + count_rows, axis=0)


def masked_scores(query, keys, ids_query, ids_keys):
    scores = jnp.einsum(
        "rqhd,rkhd->rhqk", split_heads(query), split_heads(keys), preferred_element_type=jnp.float32
    ) * HEAD_DIM ** (-0.5)
    same = ids_query[:, None, :, None] == ids_keys[:, None, None, :]
    return jnp.where(same, scores, -jnp.inf)


def attend_piece(carry, query, ids_query, piece):
    keys, values, ids_keys = piece
    peak, total, accum = carry
    scores = masked_scores(query, keys, ids_query, ids_keys)
    top = jnp.maximum(peak, jnp.max(scores, axis=-1))
    weights = jnp.exp(scores - top[..., None])
    total = jnp.sum(weights, axis=-1)
    update = jnp.einsum(
        "rhqk,rkhd->rqhd",
        weights.astype(jnp.bfloat16),
        split_heads(values),
        preferred_element_type=jnp.float32,
    )
    return (top, total, update.reshape(accum.shape))


def attention_forward(query, keys, values, ids_query):
    rows_here, slots, width = query.shape
    start_state = (
        jnp.full((rows_here, HEADS, slots), -1e30, jnp.float32),
        jnp.zeros((rows_here, HEADS, slots), jnp.float32),
        jnp.zeros((rows_here, slots, width), jnp.float32),
    )
    carry = attend_piece(
        start_state,
        query,
        ids_query,
        (
            lax.all_gather(keys, "blk", axis=1, tiled=True),
            lax.all_gather(values, "blk", axis=1, tiled=True),
            lax.all_gather(ids_query, "blk", axis=1, tiled=True),
        ),
    )
    return (carry[0], carry[1], carry[2], None)


def attention_back(query, out_grad, ids_query, log_total, inner, piece):
    keys, values, ids_keys = piece
    scale = HEAD_DIM ** (-0.5)
    scores = masked_scores(query, keys, ids_query, ids_keys)
    probs = jnp.exp(scores - log_total[..., None])
    prob_grad = jnp.einsum(
        "rqhd,rkhd->rhqk",
        split_heads(out_grad),
        split_heads(values),
        preferred_element_type=jnp.float32,
    )
    score_grad = (probs * (prob_grad - inner[..., None])).astype(jnp.bfloat16)
    value_grad = jnp.einsum(
        "rhqk,rqhd->rkhd",
        probs.astype(jnp.bfloat16),
        split_heads(out_grad),
        preferred_element_type=jnp.float32,
    )
    key_grad = (
        jnp.einsum(
            "rhqk,rqhd->rkhd", score_grad, split_heads(query), preferred_element_type=jnp.float32
        )
        * scale
    )
    query_grad = (
        jnp.einsum(
            "rhqk,rkhd->rqhd", score_grad, split_heads(keys), preferred_element_type=jnp.float32
        )
        * scale
    )
    return (
        query_grad.reshape(query.shape),
        key_grad.reshape(keys.shape),
        value_grad.reshape(values.shape),
    )


def local(
    inputs,
    image_index,
    keep_mask,
    first_gain,
    first_shift,
    input_weight,
    input_bias,
    output_weight,
    output_bias,
    second_gain,
    second_shift,
    up_weight,
    up_bias,
    down_weight,
    down_bias,
    cotangent,
):
    rows_local, slots, width = inputs.shape
    rows_micro = rows_local // MICRO
    count = rows_micro * slots
    blocks = lax.axis_size("blk")
    params = (
        first_gain,
        first_shift,
        input_weight,
        input_bias,
        output_weight,
        output_bias,
        second_gain,
        second_shift,
        up_weight,
        up_bias,
        down_weight,
        down_bias,
    )
    sums = [jnp.zeros(item.shape, jnp.float32) for item in params]
    results = []
    input_grads = []
    for micro in range(MICRO):
        first_row = micro * rows_micro
        rows_in = take_rows(inputs, first_row, rows_micro).astype(jnp.float32).reshape(count, width)
        out_cot = (
            take_rows(cotangent, first_row, rows_micro).astype(jnp.float32).reshape(count, width)
        )
        ids_query = take_rows(image_index, first_row, rows_micro).astype(jnp.bfloat16)
        keep = take_rows(keep_mask, first_row, rows_micro).astype(jnp.float32) / keep_rate
        keep_attn = jnp.broadcast_to(keep[:, None, 0:1], (rows_micro, slots, 1)).reshape(count, 1)
        keep_mlp = jnp.broadcast_to(keep[:, None, 1:2], (rows_micro, slots, 1)).reshape(count, 1)
        normed = norm_rows(rows_in, first_gain, first_shift).astype(jnp.bfloat16)
        mixed = jnp.dot(normed, input_weight, preferred_element_type=jnp.float32)
        query = (
            (mixed[:, :width] + input_bias[0])
            .astype(jnp.bfloat16)
            .reshape(rows_micro, slots, width)
        )
        keys = mixed[:, width : 2 * width].astype(jnp.bfloat16).reshape(rows_micro, slots, width)
        values = (
            (mixed[:, 2 * width :] + input_bias[1])
            .astype(jnp.bfloat16)
            .reshape(rows_micro, slots, width)
        )
        top, total, accum, whole = attention_forward(query, keys, values, ids_query)
        attended = (split_heads(accum) / jnp.transpose(total, (0, 2, 1))[..., None]).reshape(
            count, width
        )
        log_total = top + jnp.log(total)
        attended_low = attended.astype(jnp.bfloat16)
        branch = (
            jnp.dot(attended_low, output_weight, preferred_element_type=jnp.float32) + output_bias
        )
        middle = rows_in + keep_attn * branch
        normed_second = norm_rows(middle, second_gain, second_shift).astype(jnp.bfloat16)
        hidden = jnp.dot(normed_second, up_weight, preferred_element_type=jnp.float32) + up_bias
        active = gelu_exact(hidden).astype(jnp.bfloat16)
        branch_second = jnp.dot(active, down_weight, preferred_element_type=jnp.float32) + down_bias
        results.append(
            (middle + keep_mlp * branch_second)
            .astype(jnp.bfloat16)
            .reshape(rows_micro, slots, width)
        )
        mlp_grad = (out_cot * keep_mlp).astype(jnp.bfloat16)
        sums[10] = sums[10] + jnp.dot(active.T, mlp_grad, preferred_element_type=jnp.float32)
        sums[11] = sums[11] + jnp.sum(mlp_grad.astype(jnp.float32), axis=0)
        active_grad = jnp.dot(mlp_grad, down_weight.T, preferred_element_type=jnp.float32)
        hidden_grad = jax.vjp(gelu_exact, hidden)[1](active_grad)[0].astype(jnp.bfloat16)
        sums[8] = sums[8] + jnp.dot(
            normed_second.T, hidden_grad, preferred_element_type=jnp.float32
        )
        sums[9] = sums[9] + jnp.sum(hidden_grad.astype(jnp.float32), axis=0)
        second_in_grad = jnp.dot(hidden_grad, up_weight.T, preferred_element_type=jnp.float32)
        middle_part, second_gain_part, second_shift_part = jax.vjp(
            norm_rows, middle, second_gain, second_shift
        )[1](second_in_grad)
        sums[6] = sums[6] + second_gain_part
        sums[7] = sums[7] + second_shift_part
        middle_grad = middle_part + out_cot
        branch_grad = (middle_grad * keep_attn).astype(jnp.bfloat16)
        sums[4] = sums[4] + jnp.dot(attended_low.T, branch_grad, preferred_element_type=jnp.float32)
        sums[5] = sums[5] + jnp.sum(branch_grad.astype(jnp.float32), axis=0)
        attended_grad = jnp.dot(
            branch_grad, output_weight.T, preferred_element_type=jnp.float32
        ).astype(jnp.bfloat16)
        out_grad = attended_grad.reshape(rows_micro, slots, width)
        inner = jnp.transpose(
            jnp.sum(
                split_heads(
                    (attended_grad.astype(jnp.float32) * attended).reshape(rows_micro, slots, width)
                ),
                axis=-1,
            ),
            (0, 2, 1),
        )
        query_grad = jnp.zeros((rows_micro, slots, width), jnp.float32)
        visiting = (keys, values, ids_query)
        key_grad = jnp.zeros((rows_micro, slots, width), jnp.float32)
        value_grad = jnp.zeros((rows_micro, slots, width), jnp.float32)
        for step in range(blocks):
            query_part, key_part, value_part = attention_back(
                query, out_grad, ids_query, log_total, inner, visiting
            )
            query_grad = query_grad + query_part
            key_grad, value_grad = (
                from_behind((key_grad + key_part).astype(jnp.bfloat16), "blk", 1).astype(
                    jnp.float32
                ),
                from_behind((value_grad + value_part).astype(jnp.bfloat16), "blk", 1).astype(
                    jnp.float32
                ),
            )
            if step + 1 < blocks:
                visiting = from_behind((visiting[0], visiting[1], visiting[2]), "blk", 1)
        joined_grad = (
            jnp.concatenate([query_grad, key_grad, value_grad], axis=-1)
            .astype(jnp.bfloat16)
            .reshape(count, 3 * width)
        )
        sums[2] = sums[2] + jnp.dot(normed.T, joined_grad, preferred_element_type=jnp.float32)
        joined_sums = jnp.sum(joined_grad.astype(jnp.float32), axis=0)
        sums[3] = sums[3] + jnp.stack([joined_sums[:width], joined_sums[2 * width :]])
        first_in_grad = jnp.dot(joined_grad, input_weight.T, preferred_element_type=jnp.float32)
        rows_part, first_gain_part, first_shift_part = jax.vjp(
            norm_rows, rows_in, first_gain, first_shift
        )[1](first_in_grad)
        sums[0] = sums[0] + first_gain_part
        sums[1] = sums[1] + first_shift_part
        input_grads.append(
            (rows_part + middle_grad).astype(jnp.bfloat16).reshape(rows_micro, slots, width)
        )
    totals = lax.psum(
        (
            sums[0],
            sums[1],
            sums[2],
            sums[3],
            sums[4],
            sums[5],
            sums[6],
            sums[7],
            sums[8],
            sums[9],
            sums[10],
            sums[11],
        ),
        ("rows", "blk"),
    )
    return (
        jnp.concatenate(results, axis=0),
        jnp.concatenate(input_grads, axis=0),
        totals[0],
        totals[1],
        totals[2],
        totals[3],
        totals[4],
        totals[5],
        totals[6],
        totals[7],
        totals[8],
        totals[9],
        totals[10],
        totals[11],
    )


def solution(mesh):
    return jax.shard_map(
        local,
        mesh=mesh,
        in_specs=(
            P("rows", "blk", None),
            P("rows", "blk"),
            P("rows", None),
            P(),
            P(),
            P(),
            P(),
            P(),
            P(),
            P(),
            P(),
            P(),
            P(),
            P(),
            P(),
            P("rows", "blk", None),
        ),
        out_specs=(
            P("rows", "blk", None),
            P("rows", "blk", None),
            P(),
            P(),
            P(),
            P(),
            P(),
            P(),
            P(),
            P(),
            P(),
            P(),
            P(),
            P(),
        ),
        check_vma=False,
    )
```

profile of v0, /device:TPU:0, one launch (start us, length us, event | category | flops | bytes accessed | tf_op | source)
XLA Modules:
  0.0 1385.2 jit_solution(10690610558013519063)
XLA Ops:
  57.5 42.8 %all-gather.1 = bf16[4,288,2]{1,2,0:T(2,128)(2,1)S(1)} all-gather(bf16[1,288,2]{1,2,0:T(2,128)(2,1)S(1)} %get-tuple-element.80), channel_id=1, replica_groups=mesh['rows'=8,'blk'=4] {'blk'}, dimensions={0}, use_global_device_ids=true | all-gather | bytes 5760 | tf_op jit(solution)/shard_map/all_gather | solution.py:77
  125.9 7.4 fusion.144
  144.1 10.4 collective-permute-done.21
  185.8 7.3 fusion.146
  207.7 7.1 collective-permute-done.22
  217.2 7.3 fusion.148
  236.2 7.2 collective-permute-done.23
  245.7 7.3 fusion.150
  266.8 18.3 %fusion.139 = (f32[2,12,288]{2,1,0:T(8,128)S(1)}, f32[2,12,288,1152]{3,2,1,0:T(8,128)}) fusion(bf16[2,288,12,64]{1,3,2,0:T(8,128)(2,1)} %copy.184, bf16[2,1152,12,64]{1,3,2,0:T(8,128)(2,1)} %bitcast.272, pred[2,288,1152]{2,1,0:T(8,128)(4,1)} %broadcast_compare_fusion.1), kind=kOutput, calls=%fused_computation.290 | convolution fusion | flops 1043096832 | bytes 36965376 | tf_op jit(solution)/shard_map/rqhd,rkhd->rhqk/dot_general | solution.py:40
  285.1 13.4 fusion.2
  305.5 15.3 %bitcast_divide_fusion.1 = f32[2,288,12,64]{1,3,2,0:T(8,128)} fusion(bf16[2,1152,12,64]{1,3,2,0:T(8,128)(2,1)} %bitcast.273, f32[2,12,288,1152]{3,2,1,0:T(8,128)} %get-tuple-element.99, f32[2,12,288]{2,1,0:T(8,128)} %copy-done.98, f32[2,288,12]{1,2,0:T(8,128)} %bitcast.334), kind=kOutput, calls=%fused_computation.126 | convolution fusion | flops 1035583488 | bytes 37214208 | tf_op jit(solution)/shard_map/rhqk,rkhd->rqhd/dot_general | solution.py:54
  341.9 21.0 %convert_reduce_fusion.1 = (f32[3072]{0:T(1024)}, bf16[576,3072]{1,0:T(8,128)(2,1)S(1)}, f32[576,3072]{1,0:T(8,128)}) fusion(f32[576,3072]{1,0:T(8,128)S(1)} %fusion.129, f32[3072]{0:T(1024)S(1)} %copy-done.153, bf16[576,768]{1,0:T(8,128)(2,1)S(1)} %copy-done.94, bf16[3072,768]{1,0:T(8,128)(2,1)S(1)} %bitcast.344), kind=kOutput, calls=%fused_computation.43 | convolution fusion | flops 2850616320 | bytes 23322624 | tf_op jit(solution)/shard_map/dot_general | solution.py:204
  391.7 8.1 multiply_convert_fusion.7
  410.4 18.4 %fusion.138 = (f32[2,12,288]{2,1,0:T(8,128)S(1)}, f32[2,12,288,1152]{3,2,1,0:T(8,128)}) fusion(bf16[2,288,12,64]{1,3,2,0:T(8,128)(2,1)} %copy.190, bf16[2,1152,12,64]{1,3,2,0:T(8,128)(2,1)} %bitcast.274, pred[2,288,1152]{2,1,0:T(8,128)(4,1)} %broadcast_compare_fusion), kind=kOutput, calls=%fused_computation.289 | convolution fusion | flops 1043096832 | bytes 36965376 | tf_op jit(solution)/shard_map/rqhd,rkhd->rhqk/dot_general | solution.py:40
  428.9 8.5 multiply_convert_fusion.5
  461.9 14.0 %fusion.4 = f32[2,12,288]{2,1,0:T(8,128)} fusion(f32[2,12,288,1152]{3,2,1,0:T(8,128)} %get-tuple-element.97, f32[2,12,288]{2,1,0:T(8,128)S(1)} %broadcast_maximum_fusion), kind=kLoop, calls=%fused_computation.8 | loop fusion | flops 15918336 | bytes 31905792 | tf_op jit(solution)/shard_map/reduce_sum | solution.py:53
  481.7 15.4 %bitcast_divide_fusion = f32[2,288,12,64]{1,3,2,0:T(8,128)} fusion(bf16[2,1152,12,64]{1,3,2,0:T(8,128)(2,1)} %bitcast.275, f32[2,12,288,1152]{3,2,1,0:T(8,128)} %get-tuple-element.97, f32[2,12,288]{2,1,0:T(8,128)} %copy-done.97, f32[2,288,12]{1,2,0:T(8,128)} %bitcast.333), kind=kOutput, calls=%fused_computation.125 | convolution fusion | flops 1035583488 | bytes 37214208 | tf_op jit(solution)/shard_map/rhqk,rkhd->rqhd/dot_general | solution.py:54
  516.0 21.1 %convert_reduce_fusion = (f32[3072]{0:T(1024)}, bf16[576,3072]{1,0:T(8,128)(2,1)S(1)}, f32[576,3072]{1,0:T(8,128)}) fusion(f32[576,3072]{1,0:T(8,128)S(1)} %fusion.130, f32[3072]{0:T(1024)S(1)} %copy-done.154, bf16[576,768]{1,0:T(8,128)(2,1)S(1)} %copy-done.80, bf16[3072,768]{1,0:T(8,128)(2,1)S(1)} %bitcast.346), kind=kOutput, calls=%fused_computation.42 | convolution fusion | flops 2850616320 | bytes 23322624 | tf_op jit(solution)/shard_map/dot_general | solution.py:204
  544.9 8.5 fusion.40
  583.3 9.5 convolution_add_fusion.2
  592.8 14.3 %multiply_convert_fusion.9 = (bf16[576,3072]{1,0:T(8,128)(2,1)}, bf16[576,3072]{1,0:T(8,128)(2,1)}) fusion(f32[576,3072]{1,0:T(8,128)} %get-tuple-element.51, f32[576,3072]{1,0:T(8,128)} %copy-done.51, f32[3072]{0:T(1024)S(1)} %copy-done.155, f32[576,3072]{1,0:T(8,128)} %get-tuple-element.48, f32[576,3072]{1,0:T(8,128)} %copy-done.52), kind=kLoop, calls=%fused_computation.59 | loop fusion | flops 14155776 | bytes 35401728 | tf_op jit(solution)/shard_map/convert_element_type | solution.py:194
  663.0 9.2 collective-permute-done.10
  682.0 9.2 collective-permute-done.11
  739.6 8.1 fusion.97
  760.8 8.5 fusion.32
  776.1 9.5 multiply_convert_fusion
  798.0 9.6 multiply_convert_fusion.2
  915.9 7.5 convolution_add_fusion
  930.0 7.2 add_convert_fusion.16
  959.7 44.1 %all-reduce = (f32[768]{0:T(1024)}, f32[768]{0:T(1024)}, f32[2,768]{1,0:T(2,128)}, f32[768]{0:T(1024)}, f32[768]{0:T(1024)}, /*index=5*/f32[768]{0:T(1024)}, f32[3072]{0:T(1024)}, f32[768]{0:T(1024)}) all-reduce(f32[768]{0:T(1024)} %add.391, f32[768]{0:T(1024)} %add.392, ...), channel_id=1, replica_groups=mesh['rows'=8,'blk'=4] {'rows','blk'}, use_global_device_ids=true, to_apply=%region_24.25 | all-reduce | flops 9216 | bytes 73728 | tf_op jit(solution)/shard_map/psum | solution.py:269
  1008.6 348.8 %all-reduce.4.cloned.1.call-done = (f32[768,2304]{1,0:T(8,128)}, f32[768,768]{1,0:T(8,128)}, f32[768,3072]{1,0:T(8,128)}, f32[3072,768]{1,0:T(8,128)}) async-done(((f32[768,2304]{1,0:T(8,128)}, f32[768,768]{1,0:T(8,128)}, f32[768,3072]{1,0:T(8,128)}, f32[3072,768]{1,0:T(8,128)}), (f32[768,2304]{1,0:T(8,128)}, f32[768,768]{1,0:T(8,128)}, f32[768,3072]{1,0:T(8,128)}, ...) | async-done | bytes 28311568 | tf_op jit(solution)/shard_map/psum | solution.py:269
  1365.4 9.3 copy.302
  (714 shorter events, 615.5 us)
Async XLA Ops:
  7.2 253.7 %all-gather.9.cloned.1.call-start = ((), (), s32[]{:S(2)}) async-start(), calls=%async_computation.1 | async-start | bytes 4423680 | tf_op jit(solution)/shard_map/all_gather | solution.py:75
  27.5 272.3 %all-gather.7.cloned.1.call-start = ((), (), s32[]{:S(2)}) async-start(), calls=%async_computation | async-start | bytes 4423680 | tf_op jit(solution)/shard_map/all_gather | solution.py:76
  34.6 369.9 %all-gather.13.cloned.1.call-start = ((), (), s32[]{:S(2)}) async-start(), calls=%async_computation.3 | async-start | bytes 4423680 | tf_op jit(solution)/shard_map/all_gather | solution.py:75
  37.2 438.7 %all-gather.11.cloned.1.call-start = ((), (), s32[]{:S(2)}) async-start(), calls=%async_computation.2 | async-start | bytes 4423680 | tf_op jit(solution)/shard_map/all_gather | solution.py:76
  37.2 136.4 %collective-permute-start = (bf16[2,288,768]{2,1,0:T(8,128)(2,1)}, bf16[2,288,768]{2,1,0:T(8,128)(2,1)}, u32[]{:S(2)}, u32[]{:S(2)}) collective-permute-start(bf16[2,288,768]{2,1,0:T(8,128)(2,1)} %bitcast.311), channel_id=1, source_target_pairs={{0,1},{1,2},{2,3},{3,0},{4,5},{5,6},{6,7},{7,4},{8,9},{9,10},{10,1... | collective-permute-start | bytes 2654216 | tf_op jit(solution)/shard_map/ppermute | solution.py:18
  37.8 138.2 %collective-permute-start.2 = (bf16[2,288,768]{2,1,0:T(8,128)(2,1)}, bf16[2,288,768]{2,1,0:T(8,128)(2,1)}, u32[]{:S(2)}, u32[]{:S(2)}) collective-permute-start(bf16[2,288,768]{2,1,0:T(8,128)(2,1)} %bitcast.307), channel_id=1, source_target_pairs={{0,1},{1,2},{2,3},{3,0},{4,5},{5,6},{6,7},{7,4},{8,9},{9,10},{10,1... | collective-permute-start | bytes 2654216 | tf_op jit(solution)/shard_map/ppermute | solution.py:18
  40.5 139.0 %collective-permute-start.17 = (bf16[2,288,768]{2,1,0:T(8,128)(2,1)}, bf16[2,288,768]{2,1,0:T(8,128)(2,1)}, u32[]{:S(2)}, u32[]{:S(2)}) collective-permute-start(bf16[2,288,768]{2,1,0:T(8,128)(2,1)} %bitcast.309), channel_id=1, source_target_pairs={{0,1},{1,2},{2,3},{3,0},{4,5},{5,6},{6,7},{7,4},{8,9},{9,10},{10,1... | collective-permute-start | bytes 2654216 | tf_op jit(solution)/shard_map/ppermute | solution.py:18
  41.1 99.0 %collective-permute-start.1 = (bf16[2,288]{1,0:T(2,128)(2,1)S(1)}, bf16[2,288]{1,0:T(2,128)(2,1)}, u32[]{:S(2)}, u32[]{:S(2)}) collective-permute-start(bf16[2,288]{1,0:T(2,128)(2,1)S(1)} %get-tuple-element.78), channel_id=1, source_target_pairs={{0,1},{1,2},{2,3},{3,0},{4,5},{5,6},{6,7},{7,4},{8,9},{9,10},{10,1... | collective-permute-start | bytes 3464 | tf_op jit(solution)/shard_map/ppermute | solution.py:18
  41.2 99.3 %collective-permute-start.18 = (bf16[2,288]{1,0:T(2,128)(2,1)S(1)}, bf16[2,288]{1,0:T(2,128)(2,1)}, u32[]{:S(2)}, u32[]{:S(2)}) collective-permute-start(bf16[2,288]{1,0:T(2,128)(2,1)S(1)} %get-tuple-element.81), channel_id=1, source_target_pairs={{0,1},{1,2},{2,3},{3,0},{4,5},{5,6},{6,7},{7,4},{8,9},{9,10},{10,1... | collective-permute-start | bytes 3464 | tf_op jit(solution)/shard_map/ppermute | solution.py:18
  41.3 1316.2 %all-reduce.4.cloned.1.call-start = ((), (), s32[]{:S(2)}) async-start(), calls=%async_computation.4 | async-start | bytes 56623104 | tf_op jit(solution)/shard_map/psum | solution.py:269
  140.5 41.3 %collective-permute-start.19 = (bf16[2,288,768]{2,1,0:T(8,128)(2,1)}, bf16[2,288,768]{2,1,0:T(8,128)(2,1)}, u32[]{:S(2)}, u32[]{:S(2)}) collective-permute-start(bf16[2,288,768]{2,1,0:T(8,128)(2,1)} %bitcast.15), channel_id=1, source_target_pairs={{0,1},{1,2},{2,3},{3,0},{4,5},{5,6},{6,7},{7,4},{8,9},{9,10},{10,1... | collective-permute-start | bytes 2654216 | tf_op jit(solution)/shard_map/ppermute | solution.py:18
  173.7 24.9 %collective-permute-start.3 = (bf16[2,288,768]{2,1,0:T(8,128)(2,1)}, bf16[2,288,768]{2,1,0:T(8,128)(2,1)}, u32[]{:S(2)}, u32[]{:S(2)}) collective-permute-start(bf16[2,288,768]{2,1,0:T(8,128)(2,1)} %collective-permute-done), channel_id=1, source_target_pairs={{0,1},{1,2},{2,3},{3,0},{4,5},{5,6},{6,7},{7,4},{8,9},{9,10},{10,1... | collective-permute-start | bytes 2654216 | tf_op jit(solution)/shard_map/ppermute | solution.py:18
  176.0 24.9 %collective-permute-start.5 = (bf16[2,288,768]{2,1,0:T(8,128)(2,1)}, bf16[2,288,768]{2,1,0:T(8,128)(2,1)}, u32[]{:S(2)}, u32[]{:S(2)}) collective-permute-start(bf16[2,288,768]{2,1,0:T(8,128)(2,1)} %collective-permute-done.2), channel_id=1, source_target_pairs={{0,1},{1,2},{2,3},{3,0},{4,5},{5,6},{6,7},{7,4},{8,9},{9,10},{10,1... | collective-permute-start | bytes 2654216 | tf_op jit(solution)/shard_map/ppermute | solution.py:18
  179.5 25.9 %collective-permute-start.20 = (bf16[2,288,768]{2,1,0:T(8,128)(2,1)}, bf16[2,288,768]{2,1,0:T(8,128)(2,1)}, u32[]{:S(2)}, u32[]{:S(2)}) collective-permute-start(bf16[2,288,768]{2,1,0:T(8,128)(2,1)} %collective-permute-done.17), channel_id=1, source_target_pairs={{0,1},{1,2},{2,3},{3,0},{4,5},{5,6},{6,7},{7,4},{8,9},{9,10},{10,1... | collective-permute-start | bytes 2654216 | tf_op jit(solution)/shard_map/ppermute | solution.py:18
  181.8 33.0 %collective-permute-start.22 = (bf16[2,288,768]{2,1,0:T(8,128)(2,1)}, bf16[2,288,768]{2,1,0:T(8,128)(2,1)}, u32[]{:S(2)}, u32[]{:S(2)}) collective-permute-start(bf16[2,288,768]{2,1,0:T(8,128)(2,1)} %collective-permute-done.19), channel_id=1, source_target_pairs={{0,1},{1,2},{2,3},{3,0},{4,5},{5,6},{6,7},{7,4},{8,9},{9,10},{10,1... | collective-permute-start | bytes 2654216 | tf_op jit(solution)/shard_map/ppermute | solution.py:18
  198.6 31.5 %collective-permute-start.6 = (bf16[2,288,768]{2,1,0:T(8,128)(2,1)}, bf16[2,288,768]{2,1,0:T(8,128)(2,1)}, u32[]{:S(2)}, u32[]{:S(2)}) collective-permute-start(bf16[2,288,768]{2,1,0:T(8,128)(2,1)} %collective-permute-done.3), channel_id=1, source_target_pairs={{0,1},{1,2},{2,3},{3,0},{4,5},{5,6},{6,7},{7,4},{8,9},{9,10},{10,1... | collective-permute-start | bytes 2654216 | tf_op jit(solution)/shard_map/ppermute | solution.py:18
  200.9 32.9 %collective-permute-start.8 = (bf16[2,288,768]{2,1,0:T(8,128)(2,1)}, bf16[2,288,768]{2,1,0:T(8,128)(2,1)}, u32[]{:S(2)}, u32[]{:S(2)}) collective-permute-start(bf16[2,288,768]{2,1,0:T(8,128)(2,1)} %collective-permute-done.5), channel_id=1, source_target_pairs={{0,1},{1,2},{2,3},{3,0},{4,5},{5,6},{6,7},{7,4},{8,9},{9,10},{10,1... | collective-permute-start | bytes 2654216 | tf_op jit(solution)/shard_map/ppermute | solution.py:18
  205.4 37.9 %collective-permute-start.23 = (bf16[2,288,768]{2,1,0:T(8,128)(2,1)}, bf16[2,288,768]{2,1,0:T(8,128)(2,1)}, u32[]{:S(2)}, u32[]{:S(2)}) collective-permute-start(bf16[2,288,768]{2,1,0:T(8,128)(2,1)} %collective-permute-done.20), channel_id=1, source_target_pairs={{0,1},{1,2},{2,3},{3,0},{4,5},{5,6},{6,7},{7,4},{8,9},{9,10},{10,1... | collective-permute-start | bytes 2654216 | tf_op jit(solution)/shard_map/ppermute | solution.py:18
  214.9 43.7 %collective-permute-start.25 = (bf16[2,288,768]{2,1,0:T(8,128)(2,1)}, bf16[2,288,768]{2,1,0:T(8,128)(2,1)}, u32[]{:S(2)}, u32[]{:S(2)}) collective-permute-start(bf16[2,288,768]{2,1,0:T(8,128)(2,1)} %collective-permute-done.22), channel_id=1, source_target_pairs={{0,1},{1,2},{2,3},{3,0},{4,5},{5,6},{6,7},{7,4},{8,9},{9,10},{10,1... | collective-permute-start | bytes 2654216 | tf_op jit(solution)/shard_map/ppermute | solution.py:18
  544.4 104.2 %collective-permute-start.13 = (bf16[2,288,768]{2,1,0:T(8,128)(2,1)}, bf16[2,288,768]{2,1,0:T(8,128)(2,1)}, u32[]{:S(2)}, u32[]{:S(2)}) collective-permute-start(bf16[2,288,768]{2,1,0:T(8,128)(2,1)} %copy.225), channel_id=1, source_target_pairs={{0,1},{1,2},{2,3},{3,0},{4,5},{5,6},{6,7},{7,4},{8,9},{9,10},{10,1... | collective-permute-start | bytes 2654216 | tf_op jit(solution)/shard_map/ppermute | solution.py:18
  575.5 74.8 %collective-permute-start.9 = (bf16[2,288,768]{2,1,0:T(8,128)(2,1)}, bf16[2,288,768]{2,1,0:T(8,128)(2,1)}, u32[]{:S(2)}, u32[]{:S(2)}) collective-permute-start(bf16[2,288,768]{2,1,0:T(8,128)(2,1)} %copy.217), channel_id=1, source_target_pairs={{0,1},{1,2},{2,3},{3,0},{4,5},{5,6},{6,7},{7,4},{8,9},{9,10},{10,1... | collective-permute-start | bytes 2654216 | tf_op jit(solution)/shard_map/ppermute | solution.py:18
  651.9 20.3 %collective-permute-start.10 = (bf16[2,288,768]{2,1,0:T(8,128)(2,1)S(1)}, bf16[2,288,768]{2,1,0:T(8,128)(2,1)S(1)}, u32[]{:S(2)}, u32[]{:S(2)}) collective-permute-start(bf16[2,288,768]{2,1,0:T(8,128)(2,1)S(1)} %add_convert_fusion.15), channel_id=1, source_target_pairs={{0,1},{1,2},{2,3},{3,0},{4,5},{5,6},{6,7},{7,4},{8,9},{9,10},{10,1... | collective-permute-start | bytes 2654216 | tf_op jit(solution)/shard_map/ppermute | solution.py:18
  662.9 18.7 %collective-permute-start.15 = (bf16[2,288,768]{2,1,0:T(8,128)(2,1)S(1)}, bf16[2,288,768]{2,1,0:T(8,128)(2,1)S(1)}, u32[]{:S(2)}, u32[]{:S(2)}) collective-permute-start(bf16[2,288,768]{2,1,0:T(8,128)(2,1)S(1)} %add_convert_fusion.11), channel_id=1, source_target_pairs={{0,1},{1,2},{2,3},{3,0},{4,5},{5,6},{6,7},{7,4},{8,9},{9,10},{10,1... | collective-permute-start | bytes 2654216 | tf_op jit(solution)/shard_map/ppermute | solution.py:18
  681.9 18.7 %collective-permute-start.16 = (bf16[2,288,768]{2,1,0:T(8,128)(2,1)S(1)}, bf16[2,288,768]{2,1,0:T(8,128)(2,1)S(1)}, u32[]{:S(2)}, u32[]{:S(2)}) collective-permute-start(bf16[2,288,768]{2,1,0:T(8,128)(2,1)S(1)} %add_convert_fusion.10), channel_id=1, source_target_pairs={{0,1},{1,2},{2,3},{3,0},{4,5},{5,6},{6,7},{7,4},{8,9},{9,10},{10,1... | collective-permute-start | bytes 2654216 | tf_op jit(solution)/shard_map/ppermute | solution.py:18
  750.0 87.3 %collective-permute-start.30 = (bf16[2,288,768]{2,1,0:T(8,128)(2,1)}, bf16[2,288,768]{2,1,0:T(8,128)(2,1)}, u32[]{:S(2)}, u32[]{:S(2)}) collective-permute-start(bf16[2,288,768]{2,1,0:T(8,128)(2,1)} %copy.267), channel_id=1, source_target_pairs={{0,1},{1,2},{2,3},{3,0},{4,5},{5,6},{6,7},{7,4},{8,9},{9,10},{10,1... | collective-permute-start | bytes 2654216 | tf_op jit(solution)/shard_map/ppermute | solution.py:18
  819.3 20.5 %collective-permute-start.26 = (bf16[2,288,768]{2,1,0:T(8,128)(2,1)}, bf16[2,288,768]{2,1,0:T(8,128)(2,1)}, u32[]{:S(2)}, u32[]{:S(2)}) collective-permute-start(bf16[2,288,768]{2,1,0:T(8,128)(2,1)} %copy.259), channel_id=1, source_target_pairs={{0,1},{1,2},{2,3},{3,0},{4,5},{5,6},{6,7},{7,4},{8,9},{9,10},{10,1... | collective-permute-start | bytes 2654216 | tf_op jit(solution)/shard_map/ppermute | solution.py:18
  839.8 21.6 %collective-permute-start.31 = (bf16[2,288,768]{2,1,0:T(8,128)(2,1)}, bf16[2,288,768]{2,1,0:T(8,128)(2,1)}, u32[]{:S(2)}, u32[]{:S(2)}) collective-permute-start(bf16[2,288,768]{2,1,0:T(8,128)(2,1)} %add_convert_fusion.5), channel_id=1, source_target_pairs={{0,1},{1,2},{2,3},{3,0},{4,5},{5,6},{6,7},{7,4},{8,9},{9,10},{10,1... | collective-permute-start | bytes 2654216 | tf_op jit(solution)/shard_map/ppermute | solution.py:18
  842.2 21.8 %collective-permute-start.27 = (bf16[2,288,768]{2,1,0:T(8,128)(2,1)}, bf16[2,288,768]{2,1,0:T(8,128)(2,1)}, u32[]{:S(2)}, u32[]{:S(2)}) collective-permute-start(bf16[2,288,768]{2,1,0:T(8,128)(2,1)} %add_convert_fusion.8), channel_id=1, source_target_pairs={{0,1},{1,2},{2,3},{3,0},{4,5},{5,6},{6,7},{7,4},{8,9},{9,10},{10,1... | collective-permute-start | bytes 2654216 | tf_op jit(solution)/shard_map/ppermute | solution.py:18
  863.9 19.8 %collective-permute-start.32 = (bf16[2,288,768]{2,1,0:T(8,128)(2,1)}, bf16[2,288,768]{2,1,0:T(8,128)(2,1)}, u32[]{:S(2)}, u32[]{:S(2)}) collective-permute-start(bf16[2,288,768]{2,1,0:T(8,128)(2,1)} %add_convert_fusion.4), channel_id=1, source_target_pairs={{0,1},{1,2},{2,3},{3,0},{4,5},{5,6},{6,7},{7,4},{8,9},{9,10},{10,1... | collective-permute-start | bytes 2654216 | tf_op jit(solution)/shard_map/ppermute | solution.py:18
  866.4 20.0 %collective-permute-start.28 = (bf16[2,288,768]{2,1,0:T(8,128)(2,1)}, bf16[2,288,768]{2,1,0:T(8,128)(2,1)}, u32[]{:S(2)}, u32[]{:S(2)}) collective-permute-start(bf16[2,288,768]{2,1,0:T(8,128)(2,1)} %add_convert_fusion.7), channel_id=1, source_target_pairs={{0,1},{1,2},{2,3},{3,0},{4,5},{5,6},{6,7},{7,4},{8,9},{9,10},{10,1... | collective-permute-start | bytes 2654216 | tf_op jit(solution)/shard_map/ppermute | solution.py:18
  886.2 18.9 %collective-permute-start.33 = (bf16[2,288,768]{2,1,0:T(8,128)(2,1)}, bf16[2,288,768]{2,1,0:T(8,128)(2,1)}, u32[]{:S(2)}, u32[]{:S(2)}) collective-permute-start(bf16[2,288,768]{2,1,0:T(8,128)(2,1)} %add_convert_fusion.3), channel_id=1, source_target_pairs={{0,1},{1,2},{2,3},{3,0},{4,5},{5,6},{6,7},{7,4},{8,9},{9,10},{10,1... | collective-permute-start | bytes 2654216 | tf_op jit(solution)/shard_map/ppermute | solution.py:18
  888.9 19.5 %collective-permute-start.29 = (bf16[2,288,768]{2,1,0:T(8,128)(2,1)}, bf16[2,288,768]{2,1,0:T(8,128)(2,1)}, u32[]{:S(2)}, u32[]{:S(2)}) collective-permute-start(bf16[2,288,768]{2,1,0:T(8,128)(2,1)} %add_convert_fusion.6), channel_id=1, source_target_pairs={{0,1},{1,2},{2,3},{3,0},{4,5},{5,6},{6,7},{7,4},{8,9},{9,10},{10,1... | collective-permute-start | bytes 2654216 | tf_op jit(solution)/shard_map/ppermute | solution.py:18
  (211 other events, 2000.8 us)
Sparse Core Ops, SparseCore 0:
  27.6 42.8 all-gather.8
  72.7 35.8 all-gather.6
  110.1 30.7 all-gather.12
  142.3 31.4 all-gather.10
  923.6 433.7 all-reduce.3
where the time goes:
time: 1400 us; the launch traced here: 1390 us
  matrix products  450 us (32%)
  waiting for transfers between devices  419 us (30%)
  local copies, waits for them, and re-layouts  259 us (18%)
  other arithmetic  133 us (10%)
  blocking collectives  92.3 us (7%)
  starting transfers between devices  16.1 us (1%)
  between operations  16.1 us (1%)
    psum x1, waiting for transfers between devices, local(): lax.psum((sums[0], sums[1], sums[2], sums[3], sums[4], sums[5], sums[6],...  349 us
    dot_general x10, matrix products, masked_scores(): jnp.einsum('rqhd,rkhd->rhqk', split_heads(query), split_heads(keys), pref...  88.1 us
    ppermute x34, waiting for transfers between devices, from_behind(): return lax.ppermute(value, axis, pairs)  69.9 us
    another operation x16, local copies, waits for them, and re-layouts, split_heads(): return block.reshape(block.shape[0], block.shape[1], HEADS, HEAD_DIM)  65.4 us
    dot_general x8, matrix products, attention_back(): jnp.einsum('rqhd,rkhd->rhqk', split_heads(out_grad), split_heads(values),...  60.4 us
    dot_general x8, matrix products, attention_back(): jnp.einsum('rhqk,rqhd->rkhd', probs.astype(jnp.bfloat16), split_heads(out...  51 us
    all_gather x2, blocking collectives, attention_forward(): lax.all_gather(ids_query, 'blk', axis=1, tiled=True)  48.2 us
    psum x1, blocking collectives, local(): lax.psum((sums[0], sums[1], sums[2], sums[3], sums[4], sums[5], sums[6],...  44.1 us
  transfers between devices with their start and end apart: 39, of which 15 were waited for; matrix products, arithmetic and copies ran while one was open for 48% of the time, Pallas kernels for 0%

commit v1 on v0

--- a/solution.py
+++ b/solution.py
@@ -1,15 +1,453 @@
+import functools
+
 import jax
 import jax.numpy as jnp
 from jax import lax
+from jax.experimental import pallas as pl
+from jax.experimental.pallas import tpu as pltpu
 from jax.sharding import PartitionSpec as P
 
 HEADS = 12
 HEAD_DIM = 64
-MICRO = 2
-
-
+PAIR = 2 * HEAD_DIM
+PAIRS = HEADS // 2
 eps_norm = 1e-06
 keep_rate = 0.9
+F32 = jnp.float32
+BF16 = jnp.bfloat16
+NEG = -1e30
+VMEM = 62 * 1024 * 1024
+
+
+def dot(a, b):
+    return jnp.dot(a, b, preferred_element_type=F32)
+
+
+def dot_nt(a, b):
+    return lax.dot_general(a, b, (((1,), (1,)), ((), ())), preferred_element_type=F32)
+
+
+def dot_tn(a, b):
+    return lax.dot_general(a, b, (((0,), (0,)), ((), ())), preferred_element_type=F32)
+
+
+def whole(shape):
+    return pl.BlockSpec(shape, lambda *g: (0,) * len(shape), pipeline_mode=pl.Buffered(1))
+
+
+def centre_scale(values):
+    centre = values - jnp.mean(values, axis=-1, keepdims=True)
+    spread = jnp.mean(centre * centre, axis=-1, keepdims=True)
+    inv = lax.rsqrt(spread + eps_norm)
+    return centre * inv, inv
+
+
+def norm_back(grad_hat, hat, inv):
+    first = jnp.mean(grad_hat, axis=-1, keepdims=True)
+    second = jnp.mean(grad_hat * hat, axis=-1, keepdims=True)
+    return (grad_hat - first - hat * second) * inv
+
+
+def sort_tile(rank_row, tile, step, pieces):
+    span = pieces[0].shape[0]
+    place = step * tile + lax.broadcasted_iota(jnp.int32, (tile, span), 0)
+    total = None
+    for i, piece in enumerate(pieces):
+        pick = (rank_row[:, i * span : (i + 1) * span] == place).astype(BF16)
+        part = dot(pick, piece[...])
+        total = part if total is None else total + part
+    return total
+
+
+def qkv_kernel(n, tile, *refs):
+    rank, *pieces = refs[: n + 1]
+    gain, shift, weight, bias, xs_out, normed_out, qkv_out = refs[n + 1 :]
+    xs = sort_tile(rank[...], tile, pl.program_id(0), pieces)
+    xs_out[...] = xs.astype(BF16)
+    hat, _ = centre_scale(xs)
+    normed = (hat * gain[...] + shift[...]).astype(BF16)
+    normed_out[...] = normed
+    width = 3 * PAIR
+    for p in range(PAIRS):
+        cols = pl.ds(p * width, width)
+        mixed = (dot(normed, weight[:, cols]) + bias[:, cols]).astype(BF16)
+        qkv_out[:, p * width : p * width + PAIR] = mixed[:, :PAIR] * BF16(HEAD_DIM**-0.5)
+        qkv_out[:, p * width + PAIR : (p + 1) * width] = mixed[:, PAIR:]
+
+
+def qkv_call(rank, pieces, gain, shift, weight, bias, tile=288):
+    n = len(pieces)
+    span, width = pieces[0].shape
+    count = n * span
+    return pl.pallas_call(
+        functools.partial(qkv_kernel, n, tile),
+        grid=(count // tile,),
+        in_specs=[whole((1, count))]
+        + [whole((span, width))] * n
+        + [whole((1, width)), whole((1, width)), whole(weight.shape), whole(bias.shape)],
+        out_specs=[
+            pl.BlockSpec((tile, width), lambda i: (i, 0)),
+            pl.BlockSpec((tile, width), lambda i: (i, 0)),
+            pl.BlockSpec((tile, 3 * width), lambda i: (i, 0)),
+        ],
+        out_shape=[
+            jax.ShapeDtypeStruct((count, width), BF16),
+            jax.ShapeDtypeStruct((count, width), BF16),
+            jax.ShapeDtypeStruct((count, 3 * width), BF16),
+        ],
+        compiler_params=pltpu.CompilerParams(vmem_limit_bytes=VMEM),
+        cost_estimate=pl.CostEstimate(
+            flops=2 * count * width * (3 * width + count), bytes_accessed=16 * count * width, transcendentals=0
+        ),
+        name="sort_qkv",
+    )(rank, *pieces, gain, shift, weight, bias)
+
+
+SMALL = 304
+LARGE = 384
+
+
+def windows(starts, seg, length):
+    first, last = starts[seg], starts[seg + 1]
+    aligned = first // 16 * 16
+    small = SMALL if seg < 4 else LARGE
+    at_small = pl.multiple_of(jnp.minimum(aligned, length - small), 16)
+    at_large = pl.multiple_of(jnp.minimum(aligned, length - LARGE), 16)
+    return first, last, small, at_small, at_large
+
+
+def inside(at, size, lanes, first, last):
+    place = at + lax.broadcasted_iota(jnp.int32, (size, lanes), 0)
+    return (place >= first) & (place < last)
+
+
+def forward_kernel(starts, qkv, out, stat):
+    length = qkv.shape[0]
+    for seg in range(5):
+        first, last, small, at_q, at_k = windows(starts, seg, length)
+        rows_q = pl.ds(at_q, small)
+        q = qkv[rows_q, 0:PAIR]
+        k = qkv[pl.ds(at_k, LARGE), PAIR : 2 * PAIR]
+        v = qkv[pl.ds(at_k, LARGE), 2 * PAIR : 3 * PAIR]
+        lane = lax.broadcasted_iota(jnp.int32, (LARGE, PAIR), 1)
+        lane_q = lax.broadcasted_iota(jnp.int32, (small, PAIR), 1)
+        low = lane < HEAD_DIM
+        seen = inside(at_k, LARGE, PAIR, first, last)
+        zero = jnp.zeros((LARGE, PAIR), BF16)
+        one = jnp.ones((LARGE, PAIR), BF16)
+        bias = jnp.where((lane == 0) & ~seen, NEG, 0.0).astype(BF16)
+        q_ext = jnp.concatenate([q, (lane_q == 0).astype(BF16)], axis=1)
+        tops, weights, mixes = [], [], []
+        for half in (low, ~low):
+            k_ext = jnp.concatenate([jnp.where(half, k, zero), bias], axis=1)
+            scores = dot_nt(q_ext, k_ext)
+            top = jnp.max(scores, axis=-1, keepdims=True)
+            tops.append(top)
+            weights.append(jnp.exp(scores - top).astype(BF16))
+            mixes.append(jnp.concatenate([jnp.where(half, v, zero), jnp.where(half, one, zero)], axis=1))
+        both = dot(jnp.concatenate(weights, axis=1), jnp.concatenate(mixes, axis=0))
+        total = both[:, PAIR:]
+        peak = jnp.where(lane_q < HEAD_DIM, tops[0], tops[1])
+        mine = inside(at_q, small, PAIR, first, last)
+        out[rows_q, :] = jnp.where(mine, both[:, :PAIR] / total, out[rows_q, :])
+        stat[rows_q, :] = jnp.where(mine, peak + jnp.log(total), stat[rows_q, :])
+
+
+def forward_call(starts, qkv):
+    count, wide = qkv.shape
+    pairs = wide // (3 * PAIR)
+    return pl.pallas_call(
+        forward_kernel,
+        grid_spec=pltpu.PrefetchScalarGridSpec(
+            num_scalar_prefetch=1,
+            grid=(pairs,),
+            in_specs=[pl.BlockSpec((count, 3 * PAIR), lambda p, s: (0, p))],
+            out_specs=[
+                pl.BlockSpec((count, PAIR), lambda p, s: (0, p)),
+                pl.BlockSpec((count, PAIR), lambda p, s: (0, p)),
+            ],
+        ),
+        out_shape=[jax.ShapeDtypeStruct((count, pairs * PAIR), F32)] * 2,
+        compiler_params=pltpu.CompilerParams(vmem_limit_bytes=VMEM),
+        cost_estimate=pl.CostEstimate(
+            flops=4 * count * 1024 * wide // 3, bytes_accessed=10 * count * wide, transcendentals=count * 400 * HEADS
+        ),
+        name="attention_forward",
+    )(starts, qkv)
+
+
+def split3(value):
+    high = value.astype(BF16)
+    rest = value - high.astype(F32)
+    mid = rest.astype(BF16)
+    return high, mid, (rest - mid.astype(F32)).astype(BF16)
+
+
+def backward_kernel(starts, qkv, grad, att, stat, out, sums):
+    length = qkv.shape[0]
+    third = lax.broadcasted_iota(jnp.int32, (PAIR, PAIR), 0) // HEAD_DIM
+    block = (third == lax.broadcasted_iota(jnp.int32, (PAIR, PAIR), 1) // HEAD_DIM).astype(BF16)
+    for seg in range(5):
+        first, last, small, at_k, at_q = windows(starts, seg, length)
+        rows_q, rows_k = pl.ds(at_q, LARGE), pl.ds(at_k, small)
+        lane_q = lax.broadcasted_iota(jnp.int32, (LARGE, PAIR), 1)
+        lane_k = lax.broadcasted_iota(jnp.int32, (small, PAIR), 1)
+        spot_q, spot_k = lane_q % HEAD_DIM, lane_k % HEAD_DIM
+        mine_q = inside(at_q, LARGE, PAIR, first, last)
+        mine_k = inside(at_k, small, PAIR, first, last)
+        zero_q = jnp.zeros((LARGE, PAIR), BF16)
+        zero_k = jnp.zeros((small, PAIR), BF16)
+        q = qkv[rows_q, 0:PAIR]
+        k = jnp.where(mine_k, qkv[rows_k, PAIR : 2 * PAIR], zero_k)
+        v = qkv[rows_k, 2 * PAIR : 3 * PAIR]
+        g = jnp.where(mine_q, grad[rows_q, :], zero_q)
+        prod = g.astype(F32) * jnp.where(mine_q, att[rows_q, :], 0.0)
+        p_high = prod.astype(BF16)
+        p_low = (prod - p_high.astype(F32)).astype(BF16)
+        inner = dot(p_high, block) + dot(p_low, block)
+        logs = jnp.where(mine_q, stat[rows_q, :], 0.0)
+
+        def spread(value, fifth):
+            a, b, c = split3(value)
+            return jnp.where(
+                spot_q == 0, a, jnp.where(spot_q == 1, b, jnp.where(spot_q == 2, c, fifth))
+            )
+
+        query_bias = jnp.where(mine_q, 0.0, NEG).astype(BF16)
+        unit = jnp.ones((LARGE, PAIR), BF16)
+        q_ext = jnp.concatenate(
+            [q, spread(logs, jnp.where(spot_q == 3, unit, jnp.where(spot_q == 4, query_bias, zero_q)))], axis=1
+        )
+        g_ext = jnp.concatenate([g, spread(inner, zero_q)], axis=1)
+        key_bias = jnp.where(mine_k, 0.0, NEG).astype(BF16)
+        minus = jnp.where(spot_k < 3, -1.0, 0.0).astype(BF16)
+        k_tail = jnp.where(
+            spot_k == 3, key_bias, jnp.where(spot_k == 4, jnp.ones((small, PAIR), BF16), minus)
+        )
+        probs, score_grads, ks, gs, qs = [], [], [], [], []
+        for h in range(2):
+            half_k = lane_k // HEAD_DIM == h
+            half_q = lane_q // HEAD_DIM == h
+            k_half = jnp.where(half_k, k, zero_k)
+            shifted = dot_nt(jnp.concatenate([k_half, jnp.where(half_k, k_tail, zero_k)], axis=1), q_ext)
+            prob = jnp.exp(shifted)
+            v_half = jnp.where(half_k, v, zero_k)
+            prob_grad = dot_nt(jnp.concatenate([v_half, jnp.where(half_k, minus, zero_k)], axis=1), g_ext)
+            probs.append(prob.astype(BF16))
+            score_grads.append((prob * prob_grad).astype(BF16))
+            ks.append(k_half)
+            gs.append(jnp.where(half_q, g, zero_q))
+            qs.append(jnp.where(half_q, q, zero_q))
+        value_grad = dot(jnp.concatenate(probs, axis=1), jnp.concatenate(gs, axis=0))
+        key_grad = dot(jnp.concatenate(score_grads, axis=1), jnp.concatenate(qs, axis=0))
+        query_grad = dot_tn(jnp.concatenate(score_grads, axis=0), jnp.concatenate(ks, axis=0))
+        query_grad = (query_grad * HEAD_DIM**-0.5).astype(BF16)
+        out[rows_q, 0:PAIR] = jnp.where(mine_q, query_grad, out[rows_q, 0:PAIR])
+        out[rows_k, PAIR : 2 * PAIR] = jnp.where(mine_k, key_grad.astype(BF16), out[rows_k, PAIR : 2 * PAIR])
+        out[rows_k, 2 * PAIR :] = jnp.where(mine_k, value_grad.astype(BF16), out[rows_k, 2 * PAIR :])
+    sums[...] = jnp.sum(out[...].astype(F32), axis=0, keepdims=True)
+
+
+def backward_call(starts, qkv, grad, att, stat, first_pair, pairs):
+    count = qkv.shape[0]
+    return pl.pallas_call(
+        backward_kernel,
+        grid_spec=pltpu.PrefetchScalarGridSpec(
+            num_scalar_prefetch=1,
+            grid=(pairs,),
+            in_specs=[pl.BlockSpec((count, 3 * PAIR), lambda p, s: (0, p + first_pair))]
+            + [pl.BlockSpec((count, PAIR), lambda p, s: (0, p + first_pair))] * 3,
+            out_specs=[
+                pl.BlockSpec((count, 3 * PAIR), lambda p, s: (0, p)),
+                pl.BlockSpec((1, 3 * PAIR), lambda p, s: (0, p)),
+            ],
+        ),
+        out_shape=[
+            jax.ShapeDtypeStruct((count, pairs * 3 * PAIR), BF16),
+            jax.ShapeDtypeStruct((1, pairs * 3 * PAIR), F32),
+        ],
+        compiler_params=pltpu.CompilerParams(vmem_limit_bytes=VMEM),
+        cost_estimate=pl.CostEstimate(
+            flops=10 * count * 1024 * pairs * PAIR, bytes_accessed=20 * count * pairs * PAIR, transcendentals=count * 400 * 2 * pairs
+        ),
+        name="attention_backward",
+    )(starts, qkv, grad, att, stat)
+
+
+ERF = (0.254829592, -0.284496736, 1.421413741, -1.453152027, 1.061405429)
+
+
+def gelu_pair(u):
+    size = jnp.abs(u)
+    t = 1.0 / (1.0 + (0.3275911 * 0.5**0.5) * size)
+    bell = jnp.exp(u * u * -0.5)
+    poly = ERF[4] * t + ERF[3]
+    for c in (ERF[2], ERF[1], ERF[0]):
+        poly = poly * t + c
+    tail = 0.5 * poly * t * bell
+    phi = jnp.where(u < 0, tail, 1.0 - tail)
+    return u * phi, phi + u * bell * 0.3989422804014327
+
+
+def mlp_kernel(n, tile, chunk, *refs):
+    keep, rank, *pieces = refs[: n + 2]
+    (
+        att, xs, out_w, up_w, down_w, vectors, up_b,
+        result, middle_grad_out, att_low_out, normed_out, active_out, hidden_out, mlp_out, branch_out, att_grad_out,
+        sums, up_sums,
+    ) = refs[n + 2 :]
+    out_b, gain, shift, down_b = (vectors[i : i + 1, :] for i in range(4))
+    keep_attn, keep_mlp = keep[0], keep[1]
+    step = pl.program_id(0)
+    cot = sort_tile(rank[...], tile, step, pieces)
+    att_low = att[...].astype(BF16)
+    att_low_out[...] = att_low
+    middle = xs[...].astype(F32) + keep_attn * (dot(att_low, out_w[...]) + out_b)
+    hat, inv = centre_scale(middle)
+    normed = (hat * gain + shift).astype(BF16)
+    normed_out[...] = normed
+    mlp_grad = (cot * keep_mlp).astype(BF16)
+    mlp_out[...] = mlp_grad
+
+    @pl.when(step == 0)
+    def _():
+        sums[...] = jnp.zeros_like(sums)
+        up_sums[...] = jnp.zeros_like(up_sums)
+
+    lift = jnp.zeros(middle.shape, F32)
+    back = jnp.zeros(middle.shape, F32)
+    for c in range(up_w.shape[1] // chunk):
+        cols = slice(c * chunk, (c + 1) * chunk)
+        u = dot(normed, up_w[:, cols]) + up_b[:, cols]
+        act, slope = gelu_pair(u)
+        act = act.astype(BF16)
+        active_out[:, cols] = act
+        lift = lift + dot(act, down_w[cols, :])
+        hidden = (dot_nt(mlp_grad, down_w[cols, :]) * slope).astype(BF16)
+        hidden_out[:, cols] = hidden
+        up_sums[:, cols] += jnp.sum(hidden.astype(F32), axis=0, keepdims=True)
+        back = back + dot_nt(hidden, up_w[:, cols])
+    result[...] = (middle + keep_mlp * (lift + down_b)).astype(BF16)
+    middle_grad = cot + norm_back(back * gain, hat, inv)
+    middle_grad_out[...] = middle_grad
+    branch = (keep_attn * middle_grad).astype(BF16)
+    branch_out[...] = branch
+    att_grad_out[...] = dot_nt(branch, out_w[...]).astype(BF16)
+    sums[0:1, :] += jnp.sum(back * hat, axis=0, keepdims=True)
+    sums[1:2, :] += jnp.sum(back, axis=0, keepdims=True)
+    sums[2:3, :] += jnp.sum(mlp_grad.astype(F32), axis=0, keepdims=True)
+    sums[3:4, :] += jnp.sum(branch.astype(F32), axis=0, keepdims=True)
+
+
+def mlp_call(keep, rank, pieces, att, xs, out_w, up_w, down_w, vectors, up_b, tile=192, chunk=512):
+    n = len(pieces)
+    span, width = pieces[0].shape
+    count = n * span
+    ff = up_w.shape[1]
+
+    def rows(w):
+        return pl.BlockSpec((tile, w), lambda i: (i, 0))
+
+    def shape(w, dtype):
+        return jax.ShapeDtypeStruct((count, w), dtype)
+
+    return pl.pallas_call(
+        functools.partial(mlp_kernel, n, tile, chunk),
+        grid=(count // tile,),
+        in_specs=[pl.BlockSpec(memory_space=pltpu.SMEM), whole((1, count))]
+        + [whole((span, width))] * n
+        + [rows(width), rows(width), whole(out_w.shape), whole(up_w.shape), whole(down_w.shape)]
+        + [whole(vectors.shape), whole(up_b.shape)],
+        out_specs=[rows(width)] * 4
+        + [rows(ff), rows(ff)]
+        + [rows(width)] * 3
+        + [pl.BlockSpec((8, width), lambda i: (0, 0)), pl.BlockSpec((1, ff), lambda i: (0, 0))],
+        out_shape=[
+            shape(width, BF16),
+            shape(width, F32),
+            shape(width, BF16),
+            shape(width, BF16),
+            shape(ff, BF16),
+            shape(ff, BF16),
+            shape(width, BF16),
+            shape(width, BF16),
+            shape(width, BF16),
+            jax.ShapeDtypeStruct((8, width), F32),
+            jax.ShapeDtypeStruct((1, ff), F32),
+        ],
+        compiler_params=pltpu.CompilerParams(vmem_limit_bytes=VMEM),
+        cost_estimate=pl.CostEstimate(
+            flops=2 * count * width * (4 * ff + 2 * width), bytes_accessed=40 * count * width, transcendentals=2 * count * ff
+        ),
+        name="mlp",
+    )(keep, rank, *pieces, att, xs, out_w, up_w, down_w, vectors, up_b)
+
+
+def input_kernel(groups, *refs):
+    gs = refs[:groups]
+    weight, xs, middle_grad, gain, out, sums = refs[groups:]
+    span = gs[0].shape[1]
+    back = None
+    for i, g in enumerate(gs):
+        part = dot_nt(g[...], weight[:, i * span : (i + 1) * span])
+        back = part if back is None else back + part
+    hat, inv = centre_scale(xs[...].astype(F32))
+    out[...] = (middle_grad[...] + norm_back(back * gain[...], hat, inv)).astype(BF16)
+
+    @pl.when(pl.program_id(0) == 0)
+    def _():
+        sums[...] = jnp.zeros_like(sums)
+
+    sums[0:1, :] += jnp.sum(back * hat, axis=0, keepdims=True)
+    sums[1:2, :] += jnp.sum(back, axis=0, keepdims=True)
+
+
+def input_call(gs, weight, xs, middle_grad, gain, tile=288):
+    count, width = xs.shape
+    return pl.pallas_call(
+        functools.partial(input_kernel, len(gs)),
+        grid=(count // tile,),
+        in_specs=[pl.BlockSpec((tile, g.shape[1]), lambda i: (i, 0)) for g in gs]
+        + [
+            whole(weight.shape),
+            pl.BlockSpec((tile, width), lambda i: (i, 0)),
+            pl.BlockSpec((tile, width), lambda i: (i, 0)),
+            whole((1, width)),
+        ],
+        out_specs=[pl.BlockSpec((tile, width), lambda i: (i, 0)), pl.BlockSpec((8, width), lambda i: (0, 0))],
+        out_shape=[jax.ShapeDtypeStruct((count, width), BF16), jax.ShapeDtypeStruct((8, width), F32)],
+        compiler_params=pltpu.CompilerParams(vmem_limit_bytes=VMEM),
+        cost_estimate=pl.CostEstimate(
+            flops=6 * count * width * width, bytes_accessed=16 * count * width, transcendentals=0
+        ),
+        name="input_backward",
+    )(*gs, weight, xs, middle_grad, gain)
+
+
+def unsort_kernel(n, rank, xs, *outs):
+    count = xs.shape[0]
+    span = count // n
+    place = lax.broadcasted_iota(jnp.int32, (span, count), 1)
+    for i, out in enumerate(outs):
+        pick = (rank[i * span : (i + 1) * span, :] == place).astype(BF16)
+        out[...] = dot(pick, xs[...]).astype(BF16)
+
+
+def unsort_call(rank_col, xs, n):
+    count, width = xs.shape
+    span = count // n
+    return pl.pallas_call(
+        functools.partial(unsort_kernel, n),
+        out_shape=[jax.ShapeDtypeStruct((span, width), BF16)] * n,
+        compiler_params=pltpu.CompilerParams(vmem_limit_bytes=VMEM),
+        cost_estimate=pl.CostEstimate(
+            flops=2 * count * width * count, bytes_accessed=6 * count * width, transcendentals=0
+        ),
+        name="unsort",
+    )(rank_col, xs)
+
+
+MICRO = 2
 
 
 def from_behind(value, axis, steps):
@@ -301,43 +739,196 @@
     )
 
 
+def swap(value, axis, bit):
+    return lax.ppermute(value, axis, [(i, i ^ bit) for i in range(lax.axis_size(axis))])
+
+
+def side(axis, bit):
+    return (lax.axis_index(axis) // bit) % 2
+
+
+def after(value, *others):
+    return lax.optimization_barrier((value, *others))[0]
+
+
+def add_low(a, b):
+    return (a.astype(F32) + b.astype(F32)).astype(BF16)
+
+
+def axis_bits(axis):
+    bits, bit = [], 1
+    while bit < lax.axis_size(axis):
+        bits.append((axis, bit))
+        bit *= 2
+    return bits
+
+
+def scatter_sum(keep, recv, order):
+    for axis, bit in order:
+        half = keep.shape[0] // 2
+        own = side(axis, bit)
+
+        def part(which, keep=keep, recv=recv, half=half):
+            return add_low(
+                lax.dynamic_slice_in_dim(keep, which * half, half, 0),
+                lax.dynamic_slice_in_dim(recv, which * half, half, 0),
+            )
+
+        recv = swap(part(1 - own), axis, bit)
+        keep = part(own)
+    return add_low(keep, recv)
+
+
+def in_order(mine, other, own, dim):
+    mine, other = jnp.expand_dims(mine, dim), jnp.expand_dims(other, dim)
+    shape = [1] * mine.ndim
+    shape[dim] = 2
+    place = lax.broadcasted_iota(jnp.int32, shape, dim)
+    return jnp.where(place == own, mine, other)
+
+
+def gather_back(block, order):
+    for axis, bit in reversed(order):
+        pair = in_order(block, swap(block, axis, bit), side(axis, bit), 0)
+        block = pair.reshape(2 * block.shape[0], block.shape[1])
+    return block
+
+
+def sum_weights(make, orders, dim):
+    own = side("blk", 1)
+    send = make(1 - own)
+    recv = swap(send, "blk", 1)
+    keep = make(own)
+    cols = keep.shape[1] // len(orders)
+    parts = []
+    for i, order in enumerate(orders):
+        cut = slice(i * cols, (i + 1) * cols)
+        parts.append(gather_back(scatter_sum(keep[:, cut], recv[:, cut], order), order))
+    block = jnp.concatenate(parts, axis=1) if len(parts) > 1 else parts[0]
+    return in_order(block, swap(block, "blk", 1), own, dim).astype(F32)
+
+
+def sum_small(value):
+    for axis, bit in axis_bits("blk") + axis_bits("rows"):
+        value = value + swap(value, axis, bit)
+    return value
+
+
+def half_cols(array, which, size):
+    return lax.dynamic_slice_in_dim(array, which * size, size, 1)
+
+
+def local_rows(
+    inputs,
+    image_index,
+    keep_mask,
+    first_gain,
+    first_shift,
+    input_weight,
+    input_bias,
+    output_weight,
+    output_bias,
+    second_gain,
+    second_shift,
+    up_weight,
+    up_bias,
+    down_weight,
+    down_bias,
+    cotangent,
+):
+    blocks, span, width = inputs.shape
+    ff = up_weight.shape[1]
+    me = lax.axis_index("blk")
+
+    def row_piece(array, s):
+        return lax.dynamic_index_in_dim(array, me ^ s, 0, keepdims=False)
+
+    ids = [row_piece(image_index, 0)] + [swap(row_piece(image_index, s), "blk", s) for s in range(1, blocks)]
+    xs_in = [row_piece(inputs, 0)] + [swap(row_piece(inputs, s), "blk", s) for s in range(1, blocks)]
+    cots = [row_piece(cotangent, 0)] + [
+        swap(after(row_piece(cotangent, s), xs_in[-1]), "blk", s) for s in range(1, blocks)
+    ]
+    ids = jnp.concatenate(ids)
+    image = jnp.where(ids < 0, 4, ids)
+    order_key = image * ids.shape[0] + jnp.arange(ids.shape[0], dtype=jnp.int32)
+    less = (order_key[None, :] < order_key[:, None]).astype(jnp.int32)
+    rank = jnp.sum(less, axis=1)
+    starts = jnp.sum((image[None, :] < jnp.arange(6, dtype=jnp.int32)[:, None]).astype(jnp.int32), axis=1)
+    keep = lax.dynamic_index_in_dim(keep_mask, me, 0, keepdims=False).astype(F32) / keep_rate
+    rank_row, rank_col = rank[None, :], rank[:, None]
+
+    paired = input_weight.reshape(width, 3, PAIRS, PAIR).transpose(0, 2, 1, 3).reshape(width, 3 * width)
+    bias = jnp.stack([input_bias[0], jnp.zeros_like(input_bias[0]), input_bias[1]])
+    bias = bias.reshape(3, PAIRS, PAIR).transpose(1, 0, 2).reshape(1, 3 * width)
+
+    xs, normed, qkv = qkv_call(rank_row, xs_in, first_gain[None], first_shift[None], paired, bias)
+    attended, stat = forward_call(starts, qkv)
+    vectors = jnp.stack([output_bias, second_gain, second_shift, down_bias])
+    (result, middle_grad, att_low, normed2, active, hidden, mlp_grad, branch, att_grad, sums2, up_sums) = mlp_call(
+        keep, rank_row, cots, attended, xs, output_weight, up_weight, down_weight, vectors, up_bias[None]
+    )
+
+    y, x = axis_bits("blk")[1:], axis_bits("rows")[:1]
+    z = axis_bits("rows")[1:]
+    low_z, high_z = z[:1], z[1:]
+    thirds = [x + low_z + y + high_z, low_z + x + y + high_z, y + x + low_z + high_z]
+    down_total = sum_weights(lambda h: dot_tn(half_cols(active, h, ff // 2), mlp_grad).astype(BF16), thirds, 0)
+    up_total = sum_weights(lambda h: dot_tn(normed2, half_cols(hidden, h, ff // 2)).astype(BF16), thirds, 1)
+    out_total = sum_weights(lambda h: dot_tn(att_low, half_cols(branch, h, width // 2)).astype(BF16), thirds[:1], 1)
+    small = sum_small(jnp.concatenate([sums2[:4], up_sums.reshape(4, width)]))
+
+    results = unsort_call(rank_col, result, blocks)
+    groups = 3
+    each = PAIRS // groups
+    grads, bias_sums, input_totals = [], [], []
+    for g in range(groups):
+        grad, col_sums = backward_call(starts, qkv, att_grad, attended, stat, g * each, each)
+        grads.append(grad)
+        bias_sums.append(col_sums)
+        total = sum_weights(
+            lambda h, grad=grad: dot_tn(normed, half_cols(grad, h, 3 * PAIR * each // 2)).astype(BF16), thirds[g : g + 1], 1
+        )
+        input_totals.append(total.reshape(width, each, 3, PAIR))
+    inputs_grad, sums1 = input_call(grads, paired, xs, middle_grad, first_gain[None])
+    back = unsort_call(rank_col, inputs_grad, blocks)
+    bias_sum = jnp.concatenate(bias_sums, axis=1).reshape(PAIRS, 3, PAIR).transpose(1, 0, 2).reshape(3, width)
+    small_last = sum_small(jnp.concatenate([sums1[:2], bias_sum]))
+    input_total = jnp.concatenate(input_totals, axis=1).transpose(0, 2, 1, 3).reshape(width, 3 * width)
+
+    def send_back(pieces):
+        home = [pieces[0]] + [swap(pieces[s], "blk", s) for s in range(1, blocks)]
+        stacked = jnp.stack(home)
+        return jnp.stack([lax.dynamic_index_in_dim(stacked, me ^ r, 0, keepdims=False) for r in range(blocks)])
+
+    return (
+        send_back(results),
+        send_back(back),
+        small_last[0],
+        small_last[1],
+        input_total,
+        jnp.stack([small_last[2], small_last[4]]),
+        out_total.reshape(width, width),
+        small[3],
+        small[0],
+        small[1],
+        up_total.reshape(width, ff),
+        small[4:].reshape(ff),
+        down_total.reshape(ff, width),
+        small[2],
+    )
+
+
 def solution(mesh):
-    return jax.shard_map(
-        local,
-        mesh=mesh,
-        in_specs=(
-            P("rows", "blk", None),
-            P("rows", "blk"),
-            P("rows", None),
-            P(),
-            P(),
-            P(),
-            P(),
-            P(),
-            P(),
-            P(),
-            P(),
-            P(),
-            P(),
-            P(),
-            P(),
-            P("rows", "blk", None),
-        ),
-        out_specs=(
-            P("rows", "blk", None),
-            P("rows", "blk", None),
-            P(),
-            P(),
-            P(),
-            P(),
-            P(),
-            P(),
-            P(),
-            P(),
-            P(),
-            P(),
-            P(),
-            P(),
-        ),
-        check_vma=False,
-    )
+    blocks, groups = mesh.shape["blk"], mesh.shape["rows"]
+
+    def run(*args):
+        whole_rows = args[0].shape[0] // groups == blocks and blocks & (blocks - 1) == 0 and groups & (groups - 1) == 0
+        return jax.shard_map(
+            local_rows if whole_rows else local,
+            mesh=mesh,
+            in_specs=(P("rows", "blk", None), P("rows", "blk"), P("rows", None)) + (P(),) * 12 + (P("rows", "blk", None),),
+            out_specs=(P("rows", "blk", None),) * 2 + (P(),) * 12,
+            check_vma=False,
+        )(*args)
+
+    return run

time: 1400 us -> 602 us (0.43)
  matrix products: 450 us -> 40.7 us
  waiting for transfers between devices: 419 us -> 121 us
  local copies, waits for them, and re-layouts: 259 us -> 87.4 us
  Pallas kernels: 0 us -> 158 us
  starting transfers between devices: 16.1 us -> 115 us
  blocking collectives: 92.3 us -> 0 us
  other arithmetic: 133 us -> 68.9 us
    dot_general x68 -> x12, matrix products: 450 us -> 40.7 us  [dot_tn(): lax.dot_general(a, b, (((0,), (0,)), ((), ())), preferred_element_type=F32)]
    psum x1 -> x0, waiting for transfers between devices: 349 us -> none  [local(): lax.psum((sums[0], sums[1], sums[2], sums[3], sums[4], sums[5], sums[6],...]
    pallas_call x0 -> x9, Pallas kernels: none -> 158 us  [the longest x1 60.2 us: mlp_call(): pl.pallas_call(functools.partial(mlp_kernel, n, tile, chunk), grid=(count...]
    ppermute x34 -> x117, starting transfers between devices: 15.9 us -> 115 us  [swap(): lax.ppermute(value, axis, [(i, i ^ bit) for i in range(lax.axis_size(axis...]
    another operation x20 -> x5, local copies, waits for them, and re-layouts: 66.6 us -> 1.82 us  [the longest x4 1.75 us: local_rows(): vectors = jnp.stack([output_bias, second_gain, second_shift, down_bias])]
    reduce_sum x17 -> x2, other arithmetic: 58.2 us -> 1.31 us  [the longest x1 0.68 us: local_rows(): rank = jnp.sum(less, axis=1)]
    ppermute x34 -> x117, waiting for transfers between devices: 69.9 us -> 121 us  [swap(): lax.ppermute(value, axis, [(i, i ^ bit) for i in range(lax.axis_size(axis...]
    all_gather x2 -> x0, blocking collectives: 48.2 us -> none  [attention_forward(): lax.all_gather(ids_query, 'blk', axis=1, tiled=True)]
  transfers between devices with their start and end apart: 39 -> 117, of which waited for: 15 -> 40; matrix products, arithmetic and copies ran while one was open for 48% -> 25% of each run, Pallas kernels for 0% -> 9%
where the time goes in v1:
time: 602 us; the launch traced here: 594 us
  Pallas kernels  158 us (26%)
  waiting for transfers between devices  121 us (20%)
  starting transfers between devices  115 us (19%)
  local copies, waits for them, and re-layouts  87.4 us (15%)
  other arithmetic  68.9 us (11%)
  matrix products  40.7 us (7%)
    ppermute x117, waiting for transfers between devices, swap(): lax.ppermute(value, axis, [(i, i ^ bit) for i in range(lax.axis_size(axis...  121 us
    ppermute x117, starting transfers between devices, swap(): lax.ppermute(value, axis, [(i, i ^ bit) for i in range(lax.axis_size(axis...  115 us
    pallas_call x1, Pallas kernels, mlp_call(): pl.pallas_call(functools.partial(mlp_kernel, n, tile, chunk), grid=(count...  60.2 us
    pallas_call x3, Pallas kernels, backward_call(): pl.pallas_call(backward_kernel, grid_spec=pltpu.PrefetchScalarGridSpec(nu...  42.5 us
    dot_general x12, matrix products, dot_tn(): lax.dot_general(a, b, (((0,), (0,)), ((), ())), preferred_element_type=F32)  40.7 us
    select_n x28, other arithmetic, in_order(): return jnp.where(place == own, mine, other)  33.8 us
    broadcast_in_dim x48, local copies, waits for them, and re-layouts, in_order(): return jnp.where(place == own, mine, other)  27.3 us
    unnamed x174, local copies, waits for them, and re-layouts  21 us
  transfers between devices with their start and end apart: 117, of which 40 were waited for; matrix products, arithmetic and copies ran while one was open for 25% of the time, Pallas kernels for 9%

profile of v1, /device:TPU:0, one launch (start us, length us, event | category | flops | bytes accessed | tf_op | source)
XLA Modules:
  0.0 594.4 jit_solution(2712313740389858962)
XLA Ops:
  30.8 4.0 copy.74.refs_7_.refs_3_
  44.3 16.7 %sort_qkv.1 = (bf16[1152,768]{1,0:T(8,128)(2,1)}, bf16[1152,768]{1,0:T(8,128)(2,1)}, bf16[1152,2304]{1,0:T(8,128)(2,1)}) custom-call(s32[1,1152]{1,0:T(1,128)} %broadcast_in_dim.1129.refs_0_.refs_1_, bf16[288,768]{1,0:T(8,128)(2,1)} %get-tuple-element.157.refs_1_, bf16[288,768]{1,0:T(8,128)(2,1)} %copy-done.68, ...), custom_call_target="tpu_custom_call" | custom-call | flops 6115295232 | bytes 14155776 | tf_op jit(solution)/shard_map/sort_qkv/pallas_call | solution.py:82
  61.0 18.0 %attention_forward.1 = (f32[1152,768]{1,0:T(8,128)}, f32[1152,768]{1,0:T(8,128)}) custom-call(s32[6]{0:T(128)} %convert_reduce_fusion.1.starts, bf16[1152,2304]{1,0:T(8,128)(2,1)} %get-tuple-element.52.qkv), custom_call_target="tpu_custom_call" | custom-call | flops 3623878656 | bytes 26542080 | tf_op jit(solution)/shard_map/attention_forward/pallas_call | solution.py:159
  80.1 60.2 %mlp.1 = (bf16[1152,768]{1,0:T(8,128)(2,1)}, f32[1152,768]{1,0:T(8,128)}, bf16[1152,768]{1,0:T(8,128)(2,1)}, bf16[1152,768]{1,0:T(8,128)(2,1)}, bf16[1152,3072]{...) custom-call(f32[2]{0:T(128)} %fusion.47.refs_0_, ...), custom_call_target="tpu_custom_call" | custom-call | flops 24461180928 | bytes 35389440 | tf_op jit(solution)/shard_map/mlp/pallas_call | solution.py:354
  140.4 3.8 convolution_convert_fusion
  146.2 14.4 %attention_backward.5 = (bf16[1152,768]{1,0:T(8,128)(2,1)}, f32[1,768]{1,0:T(1,128)}) custom-call(s32[6]{0:T(128)} %convert_reduce_fusion.1.starts, bf16[1152,2304]{1,0:T(8,128)(2,1)} %get-tuple-element.52.qkv, bf16[1152,768]{1,0:T(8,128)(2,1)} %get-tuple-element.60.grad, f32[1152,768]{1,0:T(8,128)} %get-tuple-element.53.refs_6_.att, ...), custom_call_target="tpu_custom_call" | custom-call | flops 3019898880 | bytes 5898240 | tf_op jit(solution)/shard_map/attention_backward/pallas_call | solution.py:253
  166.0 13.9 %attention_backward.4 = (bf16[1152,768]{1,0:T(8,128)(2,1)}, f32[1,768]{1,0:T(1,128)}) custom-call(s32[6]{0:T(128)} %convert_reduce_fusion.1.starts, bf16[1152,2304]{1,0:T(8,128)(2,1)} %get-tuple-element.52.qkv, bf16[1152,768]{1,0:T(8,128)(2,1)} %get-tuple-element.60.grad, f32[1152,768]{1,0:T(8,128)} %get-tuple-element.53.refs_6_.att, ...), custom_call_target="tpu_custom_call" | custom-call | flops 3019898880 | bytes 5898240 | tf_op jit(solution)/shard_map/attention_backward/pallas_call | solution.py:253
  179.9 14.1 %attention_backward.3 = (bf16[1152,768]{1,0:T(8,128)(2,1)}, f32[1,768]{1,0:T(1,128)}) custom-call(s32[6]{0:T(128)} %convert_reduce_fusion.1.starts, bf16[1152,2304]{1,0:T(8,128)(2,1)} %get-tuple-element.52.qkv, bf16[1152,768]{1,0:T(8,128)(2,1)} %get-tuple-element.60.grad, f32[1152,768]{1,0:T(8,128)} %get-tuple-element.53.refs_6_.att, ...), custom_call_target="tpu_custom_call" | custom-call | flops 3019898880 | bytes 5898240 | tf_op jit(solution)/shard_map/attention_backward/pallas_call | solution.py:253
  194.1 6.7 %fusion.12 = bf16[768,1536]{1,0:T(8,128)(2,1)} fusion(bf16[1152,768]{1,0:T(8,128)(2,1)S(1)} %copy-done.76, bf16[1152,3072]{1,0:T(8,128)(2,1)} %get-tuple-element.81, s32[]{:T(128)S(6)} %select_n.953), kind=kOutput, calls=%fused_computation.14 | convolution fusion | flops 2719088640 | bytes 7667716 | tf_op jit(solution)/shard_map/dot_general | solution.py:31
  200.7 6.6 %fusion.9 = bf16[768,1536]{1,0:T(8,128)(2,1)} fusion(bf16[1152,768]{1,0:T(8,128)(2,1)S(1)} %copy-done.76, bf16[1152,3072]{1,0:T(8,128)(2,1)} %get-tuple-element.81, s32[]{:T(128)S(6)} %select_n.952), kind=kOutput, calls=%fused_computation.13 | convolution fusion | flops 2719088640 | bytes 7667716 | tf_op jit(solution)/shard_map/dot_general | solution.py:31
  207.4 4.6 fusion.15
  212.0 4.6 fusion.18
  221.8 11.0 %input_backward.1 = (bf16[1152,768]{1,0:T(8,128)(2,1)}, f32[8,768]{1,0:T(8,128)}) custom-call(bf16[1152,768]{1,0:T(8,128)(2,1)} %get-tuple-element.62.refs_0_, bf16[1152,768]{1,0:T(8,128)(2,1)} %get-tuple-element.63.refs_1_, bf16[1152,768]{1,0:T(8,128)(2,1)} %get-tuple-element.64.refs_2_, bf16[768,2304]{1,0:T(8,128)(2,1)} %copy.74.refs_7_.refs_3_, ...), custom_call_target="tpu_custom_call" | custom-call | flops 4076863488 | bytes 14155776 | tf_op jit(solution)/shard_map/input_backward/pallas_call | solution.py:407
  262.2 5.4 collective-permute-done.51
  306.0 4.9 unsort.2
  314.9 5.0 unsort.3
  327.4 6.8 %collective-permute-done.10 = bf16[288,768]{1,0:T(8,128)(2,1)} collective-permute-done((bf16[288,768]{1,0:T(8,128)(2,1)}, bf16[288,768]{1,0:T(8,128)(2,1)}, u32[]{:S(2)}, u32[]{:S(2)}) %collective-permute-start.10) | collective-permute-done | bytes 442400 | tf_op jit(solution)/shard_map/ppermute | solution.py:743
  334.2 8.5 %collective-permute-done.11 = bf16[288,768]{1,0:T(8,128)(2,1)} collective-permute-done((bf16[288,768]{1,0:T(8,128)(2,1)}, bf16[288,768]{1,0:T(8,128)(2,1)}, u32[]{:S(2)}, u32[]{:S(2)}) %collective-permute-start.11) | collective-permute-done | bytes 442400 | tf_op jit(solution)/shard_map/ppermute | solution.py:743
  344.7 4.1 collective-permute-done.27
  358.7 4.4 collective-permute-done.92
  370.4 4.8 collective-permute-done.82
  378.6 4.3 collective-permute-done.109
  385.8 4.8 collective-permute-done.101
  399.2 4.5 collective-permute-done.94
  438.5 4.9 collective-permute-done.69
  444.1 5.1 collective-permute-done.85
  449.2 5.2 collective-permute-done.77
  515.4 3.8 collective-permute-done.106
  562.3 8.0 %copy.89 = f32[768,2304]{1,0:T(8,128)} copy(f32[768,2304]{0,1:T(8,128)} %bitcast.257) | data formatting | bytes 14155776
  577.1 4.4 broadcast_in_dim.1308
  582.8 4.4 select_convert_fusion
  587.1 6.8 %fusion = f32[3072,768]{1,0:T(8,128)} fusion(pred[3072]{0:T(1024)(128)(4,1)S(1)} %copy-done.28, bf16[1536,768]{1,0:T(8,128)(2,1)} %collective-permute-done.116, bf16[1536,768]{1,0:T(8,128)(2,1)} %pad_maximum_fusion.1), kind=kLoop, calls=%fused_computation.2 | loop fusion | flops 4718592 | bytes 14158848 | tf_op jit(solution)/shard_map/convert_element_type | solution.py:808
  (601 shorter events, 313.1 us)
Async XLA Ops:
  2.1 35.4 %collective-permute-start.2 = (s32[288]{0:T(512)}, s32[288]{0:T(512)}, u32[]{:S(2)}, u32[]{:S(2)}) collective-permute-start(s32[288]{0:T(512)} %get-tuple-element.132), channel_id=1, source_target_pairs={{0,3},{1,2},{2,1},{3,0},{4,7},{5,6},{6,5},{7,4},{8,11},{9,10},{10,... | collective-permute-start | bytes 3464 | tf_op jit(solution)/shard_map/ppermute | solution.py:743
  4.5 33.1 %collective-permute-start = (s32[288]{0:T(512)}, s32[288]{0:T(512)}, u32[]{:S(2)}, u32[]{:S(2)}) collective-permute-start(s32[288]{0:T(512)} %get-tuple-element.133), channel_id=1, source_target_pairs={{0,1},{1,0},{2,3},{3,2},{4,5},{5,4},{6,7},{7,6},{8,9},{9,8},{10,11... | collective-permute-start | bytes 3464 | tf_op jit(solution)/shard_map/ppermute | solution.py:743
  5.3 32.4 %collective-permute-start.1 = (s32[288]{0:T(512)}, s32[288]{0:T(512)}, u32[]{:S(2)}, u32[]{:S(2)}) collective-permute-start(s32[288]{0:T(512)} %get-tuple-element.135), channel_id=1, source_target_pairs={{0,2},{1,3},{2,0},{3,1},{4,6},{5,7},{6,4},{7,5},{8,10},{9,11},{10,... | collective-permute-start | bytes 3464 | tf_op jit(solution)/shard_map/ppermute | solution.py:743
  8.0 35.6 %collective-permute-start.8 = (bf16[288,768]{1,0:T(8,128)(2,1)}, bf16[288,768]{1,0:T(8,128)(2,1)}, u32[]{:S(2)}, u32[]{:S(2)}) collective-permute-start(bf16[288,768]{1,0:T(8,128)(2,1)} %get-tuple-element.156), channel_id=1, source_target_pairs={{0,2},{1,3},{2,0},{3,1},{4,6},{5,7},{6,4},{7,5},{8,10},{9,11},{10,... | collective-permute-start | bytes 1327112 | tf_op jit(solution)/shard_map/ppermute | solution.py:743
  10.0 31.4 %collective-permute-start.3 = (bf16[288,768]{1,0:T(8,128)(2,1)}, bf16[288,768]{1,0:T(8,128)(2,1)}, u32[]{:S(2)}, u32[]{:S(2)}) collective-permute-start(bf16[288,768]{1,0:T(8,128)(2,1)} %get-tuple-element.158), channel_id=1, source_target_pairs={{0,3},{1,2},{2,1},{3,0},{4,7},{5,6},{6,5},{7,4},{8,11},{9,10},{10,... | collective-permute-start | bytes 1327112 | tf_op jit(solution)/shard_map/ppermute | solution.py:743
  41.4 37.6 %collective-permute-start.5 = (bf16[288,768]{1,0:T(8,128)(2,1)}, bf16[288,768]{1,0:T(8,128)(2,1)S(1)}, u32[]{:S(2)}, u32[]{:S(2)}) collective-permute-start(bf16[288,768]{1,0:T(8,128)(2,1)} %get-tuple-element.50), channel_id=1, source_target_pairs={{0,2},{1,3},{2,0},{3,1},{4,6},{5,7},{6,4},{7,5},{8,10},{9,11},{10,... | collective-permute-start | bytes 1327112 | tf_op jit(solution)/shard_map/ppermute | solution.py:743
  43.4 35.6 %collective-permute-start.4 = (bf16[288,768]{1,0:T(8,128)(2,1)}, bf16[288,768]{1,0:T(8,128)(2,1)S(1)}, u32[]{:S(2)}, u32[]{:S(2)}) collective-permute-start(bf16[288,768]{1,0:T(8,128)(2,1)} %get-tuple-element.49), channel_id=1, source_target_pairs={{0,1},{1,0},{2,3},{3,2},{4,5},{5,4},{6,7},{7,6},{8,9},{9,8},{10,11... | collective-permute-start | bytes 1327112 | tf_op jit(solution)/shard_map/ppermute | solution.py:743
  43.4 35.7 %collective-permute-start.6 = (bf16[288,768]{1,0:T(8,128)(2,1)}, bf16[288,768]{1,0:T(8,128)(2,1)S(1)}, u32[]{:S(2)}, u32[]{:S(2)}) collective-permute-start(bf16[288,768]{1,0:T(8,128)(2,1)} %get-tuple-element.51), channel_id=1, source_target_pairs={{0,3},{1,2},{2,1},{3,0},{4,7},{5,6},{6,5},{7,4},{8,11},{9,10},{10,... | collective-permute-start | bytes 1327112 | tf_op jit(solution)/shard_map/ppermute | solution.py:743
  217.8 39.8 %collective-permute-start.40 = (bf16[768,384]{1,0:T(8,128)(2,1)}, bf16[768,384]{1,0:T(8,128)(2,1)}, u32[]{:S(2)}, u32[]{:S(2)}) collective-permute-start(bf16[768,384]{1,0:T(8,128)(2,1)} %convolution_convert_fusion.2), channel_id=1, source_target_pairs={{0,1},{1,0},{2,3},{3,2},{4,5},{5,4},{6,7},{7,6},{8,9},{9,8},{10,11... | collective-permute-start | bytes 1769480 | tf_op jit(solution)/shard_map/ppermute | solution.py:743
  238.5 18.4 %collective-permute-start.50 = (bf16[768,384]{1,0:T(8,128)(2,1)S(1)}, bf16[768,384]{1,0:T(8,128)(2,1)S(1)}, u32[]{:S(2)}, u32[]{:S(2)}) collective-permute-start(bf16[768,384]{1,0:T(8,128)(2,1)S(1)} %copy-done.63), channel_id=1, source_target_pairs={{0,1},{1,0},{2,3},{3,2},{4,5},{5,4},{6,7},{7,6},{8,9},{9,8},{10,11... | collective-permute-start | bytes 1769480 | tf_op jit(solution)/shard_map/ppermute | solution.py:743
  256.9 92.0 %collective-permute-start.91 = (bf16[1536,768]{1,0:T(8,128)(2,1)}, bf16[1536,768]{1,0:T(8,128)(2,1)}, u32[]{:S(2)}, u32[]{:S(2)}) collective-permute-start(bf16[1536,768]{1,0:T(8,128)(2,1)} %fusion.18), channel_id=1, source_target_pairs={{0,1},{1,0},{2,3},{3,2},{4,5},{5,4},{6,7},{7,6},{8,9},{9,8},{10,11... | collective-permute-start | bytes 7077896 | tf_op jit(solution)/shard_map/ppermute | solution.py:743
  256.9 98.5 %collective-permute-start.65 = (bf16[768,1536]{1,0:T(8,128)(2,1)}, bf16[768,1536]{1,0:T(8,128)(2,1)}, u32[]{:S(2)}, u32[]{:S(2)}) collective-permute-start(bf16[768,1536]{1,0:T(8,128)(2,1)} %fusion.12), channel_id=1, source_target_pairs={{0,1},{1,0},{2,3},{3,2},{4,5},{5,4},{6,7},{7,6},{8,9},{9,8},{10,11... | collective-permute-start | bytes 7077896 | tf_op jit(solution)/shard_map/ppermute | solution.py:743
  321.8 20.9 %collective-permute-start.11 = (bf16[288,768]{1,0:T(8,128)(2,1)}, bf16[288,768]{1,0:T(8,128)(2,1)}, u32[]{:S(2)}, u32[]{:S(2)}) collective-permute-start(bf16[288,768]{1,0:T(8,128)(2,1)} %get-tuple-element.59), channel_id=1, source_target_pairs={{0,3},{1,2},{2,1},{3,0},{4,7},{5,6},{6,5},{7,4},{8,11},{9,10},{10,... | collective-permute-start | bytes 1327112 | tf_op jit(solution)/shard_map/ppermute | solution.py:743
  344.2 110.2 %collective-permute-start.12 = (bf16[288,768]{1,0:T(8,128)(2,1)S(1)}, bf16[288,768]{1,0:T(8,128)(2,1)S(1)}, u32[]{:S(2)}, u32[]{:S(2)}) collective-permute-start(bf16[288,768]{1,0:T(8,128)(2,1)S(1)} %copy-done.67), channel_id=1, source_target_pairs={{0,1},{1,0},{2,3},{3,2},{4,5},{5,4},{6,7},{7,6},{8,9},{9,8},{10,11... | collective-permute-start | bytes 1327112 | tf_op jit(solution)/shard_map/ppermute | solution.py:743
  365.1 90.9 %collective-permute-start.13 = (bf16[288,768]{1,0:T(8,128)(2,1)S(1)}, bf16[288,768]{1,0:T(8,128)(2,1)S(1)}, u32[]{:S(2)}, u32[]{:S(2)}) collective-permute-start(bf16[288,768]{1,0:T(8,128)(2,1)S(1)} %copy-done.66), channel_id=1, source_target_pairs={{0,2},{1,3},{2,0},{3,1},{4,6},{5,7},{6,4},{7,5},{8,10},{9,11},{10,... | collective-permute-start | bytes 1327112 | tf_op jit(solution)/shard_map/ppermute | solution.py:743
  370.3 88.6 %collective-permute-start.14 = (bf16[288,768]{1,0:T(8,128)(2,1)S(1)}, bf16[288,768]{1,0:T(8,128)(2,1)S(1)}, u32[]{:S(2)}, u32[]{:S(2)}) collective-permute-start(bf16[288,768]{1,0:T(8,128)(2,1)S(1)} %copy-done.65), channel_id=1, source_target_pairs={{0,3},{1,2},{2,1},{3,0},{4,7},{5,6},{6,5},{7,4},{8,11},{9,10},{10,... | collective-permute-start | bytes 1327112 | tf_op jit(solution)/shard_map/ppermute | solution.py:743
  396.3 65.5 %collective-permute-start.37 = (bf16[192,384]{1,0:T(8,128)(2,1)S(1)}, bf16[192,384]{1,0:T(8,128)(2,1)S(1)}, u32[]{:S(2)}, u32[]{:S(2)}) collective-permute-start(bf16[192,384]{1,0:T(8,128)(2,1)S(1)} %get-tuple-element.249), channel_id=1, source_target_pairs={{0,4},{4,0},{8,12},{12,8},{16,20},{20,16},{24,28},{28,24},{1,5},{5... | collective-permute-start | bytes 442376 | tf_op jit(solution)/shard_map/ppermute | solution.py:743
  461.8 19.9 %collective-permute-start.58 = (bf16[384,384]{1,0:T(8,128)(2,1)S(1)}, bf16[384,384]{1,0:T(8,128)(2,1)S(1)}, u32[]{:S(2)}, u32[]{:S(2)}) collective-permute-start(bf16[384,384]{1,0:T(8,128)(2,1)S(1)} %get-tuple-element.246), channel_id=1, source_target_pairs={{0,4},{4,0},{8,12},{12,8},{16,20},{20,16},{24,28},{28,24},{1,5},{5... | collective-permute-start | bytes 884744 | tf_op jit(solution)/shard_map/ppermute | solution.py:743
  462.5 20.0 %collective-permute-start.28 = (bf16[384,384]{1,0:T(8,128)(2,1)S(1)}, bf16[384,384]{1,0:T(8,128)(2,1)S(1)}, u32[]{:S(2)}, u32[]{:S(2)}) collective-permute-start(bf16[384,384]{1,0:T(8,128)(2,1)S(1)} %get-tuple-element.247), channel_id=1, source_target_pairs={{0,4},{4,0},{8,12},{12,8},{16,20},{20,16},{24,28},{28,24},{1,5},{5... | collective-permute-start | bytes 884744 | tf_op jit(solution)/shard_map/ppermute | solution.py:743
  477.0 29.1 %collective-permute-start.48 = (bf16[384,384]{1,0:T(8,128)(2,1)}, bf16[384,384]{1,0:T(8,128)(2,1)}, u32[]{:S(2)}, u32[]{:S(2)}) collective-permute-start(bf16[384,384]{1,0:T(8,128)(2,1)} %get-tuple-element.259), channel_id=1, source_target_pairs={{0,2},{1,3},{2,0},{3,1},{4,6},{5,7},{6,4},{7,5},{8,10},{9,11},{10,... | collective-permute-start | bytes 884744 | tf_op jit(solution)/shard_map/ppermute | solution.py:743
  480.4 18.4 %collective-permute-start.88 = (bf16[192,512]{1,0:T(8,128)(2,1)}, bf16[192,512]{1,0:T(8,128)(2,1)}, u32[]{:S(2)}, u32[]{:S(2)}) collective-permute-start(bf16[192,512]{1,0:T(8,128)(2,1)} %bitcast_select_fusion.20), channel_id=1, source_target_pairs={{0,4},{4,0},{8,12},{12,8},{16,20},{20,16},{24,28},{28,24},{1,5},{5... | collective-permute-start | bytes 589832 | tf_op jit(solution)/shard_map/ppermute | solution.py:743
  481.8 21.1 %collective-permute-start.72 = (bf16[192,512]{1,0:T(8,128)(2,1)}, bf16[192,512]{1,0:T(8,128)(2,1)}, u32[]{:S(2)}, u32[]{:S(2)}) collective-permute-start(bf16[192,512]{1,0:T(8,128)(2,1)} %get-tuple-element.239), channel_id=1, source_target_pairs={{0,8},{4,12},{8,0},{12,4},{16,24},{20,28},{24,16},{28,20},{1,9},{5... | collective-permute-start | bytes 589832 | tf_op jit(solution)/shard_map/ppermute | solution.py:743
  485.3 21.3 %collective-permute-start.97 = (bf16[192,256]{1,0:T(8,128)(2,1)}, bf16[192,256]{1,0:T(8,128)(2,1)}, u32[]{:S(2)}, u32[]{:S(2)}) collective-permute-start(bf16[192,256]{1,0:T(8,128)(2,1)} %get-tuple-element.236), channel_id=1, source_target_pairs={{0,2},{1,3},{2,0},{3,1},{4,6},{5,7},{6,4},{7,5},{8,10},{9,11},{10,... | collective-permute-start | bytes 294920 | tf_op jit(solution)/shard_map/ppermute | solution.py:743
  502.9 21.3 %collective-permute-start.81 = (bf16[384,512]{1,0:T(8,128)(2,1)}, bf16[384,512]{1,0:T(8,128)(2,1)}, u32[]{:S(2)}, u32[]{:S(2)}) collective-permute-start(bf16[384,512]{1,0:T(8,128)(2,1)} %get-tuple-element.244), channel_id=1, source_target_pairs={{0,8},{4,12},{8,0},{12,4},{16,24},{20,28},{24,16},{28,20},{1,9},{5... | collective-permute-start | bytes 1179656 | tf_op jit(solution)/shard_map/ppermute | solution.py:743
  506.1 22.5 %collective-permute-start.89 = (bf16[384,512]{1,0:T(8,128)(2,1)}, bf16[384,512]{1,0:T(8,128)(2,1)}, u32[]{:S(2)}, u32[]{:S(2)}) collective-permute-start(bf16[384,512]{1,0:T(8,128)(2,1)} %get-tuple-element.245), channel_id=1, source_target_pairs={{0,2},{1,3},{2,0},{3,1},{4,6},{5,7},{6,4},{7,5},{8,10},{9,11},{10,... | collective-permute-start | bytes 1179656 | tf_op jit(solution)/shard_map/ppermute | solution.py:743
  506.6 20.0 %collective-permute-start.73 = (bf16[384,512]{1,0:T(8,128)(2,1)}, bf16[384,512]{1,0:T(8,128)(2,1)}, u32[]{:S(2)}, u32[]{:S(2)}) collective-permute-start(bf16[384,512]{1,0:T(8,128)(2,1)} %bitcast_select_fusion.12), channel_id=1, source_target_pairs={{0,4},{4,0},{8,12},{12,8},{16,20},{20,16},{24,28},{28,24},{1,5},{5... | collective-permute-start | bytes 1179656 | tf_op jit(solution)/shard_map/ppermute | solution.py:743
  530.2 47.0 %collective-permute-start.90 = (bf16[768,1536]{1,0:T(8,128)(2,1)S(1)}, bf16[768,1536]{1,0:T(8,128)(2,1)}, u32[]{:S(2)}, u32[]{:S(2)}) collective-permute-start(bf16[768,1536]{1,0:T(8,128)(2,1)S(1)} %pad_maximum_fusion), channel_id=1, source_target_pairs={{0,1},{1,0},{2,3},{3,2},{4,5},{5,4},{6,7},{7,6},{8,9},{9,8},{10,11... | collective-permute-start | bytes 7077896 | tf_op jit(solution)/shard_map/ppermute | solution.py:743
  531.8 18.8 %collective-permute-start.59 = (bf16[768,384]{0,1:T(8,128)(2,1)}, bf16[768,384]{0,1:T(8,128)(2,1)}, u32[]{:S(2)}, u32[]{:S(2)}) collective-permute-start(bf16[768,384]{0,1:T(8,128)(2,1)} %get-tuple-element.232), channel_id=1, source_target_pairs={{0,1},{1,0},{2,3},{3,2},{4,5},{5,4},{6,7},{7,6},{8,9},{9,8},{10,11... | collective-permute-start | bytes 1769480 | tf_op jit(solution)/shard_map/ppermute | solution.py:743
  538.7 18.5 %collective-permute-start.39 = (bf16[768,384]{0,1:T(8,128)(2,1)}, bf16[768,384]{0,1:T(8,128)(2,1)}, u32[]{:S(2)}, u32[]{:S(2)}) collective-permute-start(bf16[768,384]{0,1:T(8,128)(2,1)} %broadcast_select_fusion.5), channel_id=1, source_target_pairs={{0,1},{1,0},{2,3},{3,2},{4,5},{5,4},{6,7},{7,6},{8,9},{9,8},{10,11... | collective-permute-start | bytes 1769480 | tf_op jit(solution)/shard_map/ppermute | solution.py:743
  538.7 18.5 %collective-permute-start.49 = (bf16[768,384]{0,1:T(8,128)(2,1)}, bf16[768,384]{0,1:T(8,128)(2,1)}, u32[]{:S(2)}, u32[]{:S(2)}) collective-permute-start(bf16[768,384]{0,1:T(8,128)(2,1)} %broadcast_select_fusion.3), channel_id=1, source_target_pairs={{0,1},{1,0},{2,3},{3,2},{4,5},{5,4},{6,7},{7,6},{8,9},{9,8},{10,11... | collective-permute-start | bytes 1769480 | tf_op jit(solution)/shard_map/ppermute | solution.py:743
  539.2 18.0 %collective-permute-start.29 = (bf16[768,384]{0,1:T(8,128)(2,1)}, bf16[768,384]{0,1:T(8,128)(2,1)}, u32[]{:S(2)}, u32[]{:S(2)}) collective-permute-start(bf16[768,384]{0,1:T(8,128)(2,1)} %get-tuple-element.233), channel_id=1, source_target_pairs={{0,1},{1,0},{2,3},{3,2},{4,5},{5,4},{6,7},{7,6},{8,9},{9,8},{10,11... | collective-permute-start | bytes 1769480 | tf_op jit(solution)/shard_map/ppermute | solution.py:743
  550.6 36.5 %collective-permute-start.116 = (bf16[1536,768]{1,0:T(8,128)(2,1)}, bf16[1536,768]{1,0:T(8,128)(2,1)}, u32[]{:S(2)}, u32[]{:S(2)}) collective-permute-start(bf16[1536,768]{1,0:T(8,128)(2,1)} %pad_maximum_fusion.1), channel_id=1, source_target_pairs={{0,1},{1,0},{2,3},{3,2},{4,5},{5,4},{6,7},{7,6},{8,9},{9,8},{10,11... | collective-permute-start | bytes 7077896 | tf_op jit(solution)/shard_map/ppermute | solution.py:743
  (165 other events, 1284.8 us)

commit v2 on v1

--- a/solution.py
+++ b/solution.py
@@ -17,6 +17,7 @@
 BF16 = jnp.bfloat16
 NEG = -1e30
 VMEM = 62 * 1024 * 1024
+QUICK = pl.CostEstimate(flops=1 << 20, bytes_accessed=1 << 16, transcendentals=0)
 
 
 def dot(a, b):
@@ -67,12 +68,11 @@
     hat, _ = centre_scale(xs)
     normed = (hat * gain[...] + shift[...]).astype(BF16)
     normed_out[...] = normed
-    width = 3 * PAIR
-    for p in range(PAIRS):
-        cols = pl.ds(p * width, width)
-        mixed = (dot(normed, weight[:, cols]) + bias[:, cols]).astype(BF16)
-        qkv_out[:, p * width : p * width + PAIR] = mixed[:, :PAIR] * BF16(HEAD_DIM**-0.5)
-        qkv_out[:, p * width + PAIR : (p + 1) * width] = mixed[:, PAIR:]
+    width = normed.shape[1]
+    for j in range(3):
+        cols = slice(j * width, (j + 1) * width)
+        mixed = (dot(normed, weight[:, cols]) + bias[j : j + 1, :]).astype(BF16)
+        qkv_out[j] = mixed * BF16(HEAD_DIM**-0.5) if j == 0 else mixed
 
 
 def qkv_call(rank, pieces, gain, shift, weight, bias, tile=288):
@@ -88,17 +88,15 @@
         out_specs=[
             pl.BlockSpec((tile, width), lambda i: (i, 0)),
             pl.BlockSpec((tile, width), lambda i: (i, 0)),
-            pl.BlockSpec((tile, 3 * width), lambda i: (i, 0)),
+            pl.BlockSpec((3, tile, width), lambda i: (0, i, 0)),
         ],
         out_shape=[
             jax.ShapeDtypeStruct((count, width), BF16),
             jax.ShapeDtypeStruct((count, width), BF16),
-            jax.ShapeDtypeStruct((count, 3 * width), BF16),
+            jax.ShapeDtypeStruct((3, count, width), BF16),
         ],
         compiler_params=pltpu.CompilerParams(vmem_limit_bytes=VMEM),
-        cost_estimate=pl.CostEstimate(
-            flops=2 * count * width * (3 * width + count), bytes_accessed=16 * count * width, transcendentals=0
-        ),
+        cost_estimate=QUICK,
         name="sort_qkv",
     )(rank, *pieces, gain, shift, weight, bias)
 
@@ -122,13 +120,13 @@
 
 
 def forward_kernel(starts, qkv, out, stat):
-    length = qkv.shape[0]
+    length = qkv.shape[1]
     for seg in range(5):
         first, last, small, at_q, at_k = windows(starts, seg, length)
         rows_q = pl.ds(at_q, small)
-        q = qkv[rows_q, 0:PAIR]
-        k = qkv[pl.ds(at_k, LARGE), PAIR : 2 * PAIR]
-        v = qkv[pl.ds(at_k, LARGE), 2 * PAIR : 3 * PAIR]
+        q = qkv[0, rows_q, :]
+        k = qkv[1, pl.ds(at_k, LARGE), :]
+        v = qkv[2, pl.ds(at_k, LARGE), :]
         lane = lax.broadcasted_iota(jnp.int32, (LARGE, PAIR), 1)
         lane_q = lax.broadcasted_iota(jnp.int32, (small, PAIR), 1)
         low = lane < HEAD_DIM
@@ -154,14 +152,14 @@
 
 
 def forward_call(starts, qkv):
-    count, wide = qkv.shape
-    pairs = wide // (3 * PAIR)
+    _, count, wide = qkv.shape
+    pairs = wide // PAIR
     return pl.pallas_call(
         forward_kernel,
         grid_spec=pltpu.PrefetchScalarGridSpec(
             num_scalar_prefetch=1,
             grid=(pairs,),
-            in_specs=[pl.BlockSpec((count, 3 * PAIR), lambda p, s: (0, p))],
+            in_specs=[pl.BlockSpec((3, count, PAIR), lambda p, s: (0, 0, p))],
             out_specs=[
                 pl.BlockSpec((count, PAIR), lambda p, s: (0, p)),
                 pl.BlockSpec((count, PAIR), lambda p, s: (0, p)),
@@ -169,9 +167,7 @@
         ),
         out_shape=[jax.ShapeDtypeStruct((count, pairs * PAIR), F32)] * 2,
         compiler_params=pltpu.CompilerParams(vmem_limit_bytes=VMEM),
-        cost_estimate=pl.CostEstimate(
-            flops=4 * count * 1024 * wide // 3, bytes_accessed=10 * count * wide, transcendentals=count * 400 * HEADS
-        ),
+        cost_estimate=QUICK,
         name="attention_forward",
     )(starts, qkv)
 
@@ -183,8 +179,9 @@
     return high, mid, (rest - mid.astype(F32)).astype(BF16)
 
 
-def backward_kernel(starts, qkv, grad, att, stat, out, sums):
-    length = qkv.shape[0]
+def backward_kernel(starts, qkv, grad, att, stat, *refs):
+    out, sums = refs[-2:]
+    length = qkv.shape[1]
     third = lax.broadcasted_iota(jnp.int32, (PAIR, PAIR), 0) // HEAD_DIM
     block = (third == lax.broadcasted_iota(jnp.int32, (PAIR, PAIR), 1) // HEAD_DIM).astype(BF16)
     for seg in range(5):
@@ -197,9 +194,9 @@
         mine_k = inside(at_k, small, PAIR, first, last)
         zero_q = jnp.zeros((LARGE, PAIR), BF16)
         zero_k = jnp.zeros((small, PAIR), BF16)
-        q = qkv[rows_q, 0:PAIR]
-        k = jnp.where(mine_k, qkv[rows_k, PAIR : 2 * PAIR], zero_k)
-        v = qkv[rows_k, 2 * PAIR : 3 * PAIR]
+        q = qkv[0, rows_q, :]
+        k = jnp.where(mine_k, qkv[1, rows_k, :], zero_k)
+        v = qkv[2, rows_k, :]
         g = jnp.where(mine_q, grad[rows_q, :], zero_q)
         prod = g.astype(F32) * jnp.where(mine_q, att[rows_q, :], 0.0)
         p_high = prod.astype(BF16)
@@ -242,36 +239,38 @@
         key_grad = dot(jnp.concatenate(score_grads, axis=1), jnp.concatenate(qs, axis=0))
         query_grad = dot_tn(jnp.concatenate(score_grads, axis=0), jnp.concatenate(ks, axis=0))
         query_grad = (query_grad * HEAD_DIM**-0.5).astype(BF16)
-        out[rows_q, 0:PAIR] = jnp.where(mine_q, query_grad, out[rows_q, 0:PAIR])
-        out[rows_k, PAIR : 2 * PAIR] = jnp.where(mine_k, key_grad.astype(BF16), out[rows_k, PAIR : 2 * PAIR])
-        out[rows_k, 2 * PAIR :] = jnp.where(mine_k, value_grad.astype(BF16), out[rows_k, 2 * PAIR :])
-    sums[...] = jnp.sum(out[...].astype(F32), axis=0, keepdims=True)
-
-
-def backward_call(starts, qkv, grad, att, stat, first_pair, pairs):
-    count = qkv.shape[0]
+        out[0, rows_q, :] = jnp.where(mine_q, query_grad, out[0, rows_q, :])
+        out[1, rows_k, :] = jnp.where(mine_k, key_grad.astype(BF16), out[1, rows_k, :])
+        out[2, rows_k, :] = jnp.where(mine_k, value_grad.astype(BF16), out[2, rows_k, :])
+    for j in range(3):
+        sums[j : j + 1, :] = jnp.sum(out[j].astype(F32), axis=0, keepdims=True)
+
+
+def backward_call(starts, qkv, grad, att, stat, first_pair, pairs, before=None):
+    _, count, width = qkv.shape
+    held = [] if before is None else list(before)
     return pl.pallas_call(
         backward_kernel,
         grid_spec=pltpu.PrefetchScalarGridSpec(
             num_scalar_prefetch=1,
             grid=(pairs,),
-            in_specs=[pl.BlockSpec((count, 3 * PAIR), lambda p, s: (0, p + first_pair))]
-            + [pl.BlockSpec((count, PAIR), lambda p, s: (0, p + first_pair))] * 3,
+            in_specs=[pl.BlockSpec((3, count, PAIR), lambda p, s: (0, 0, p + first_pair))]
+            + [pl.BlockSpec((count, PAIR), lambda p, s: (0, p + first_pair))] * 3
+            + [pl.BlockSpec(memory_space=pl.ANY)] * len(held),
             out_specs=[
-                pl.BlockSpec((count, 3 * PAIR), lambda p, s: (0, p)),
-                pl.BlockSpec((1, 3 * PAIR), lambda p, s: (0, p)),
+                pl.BlockSpec((3, count, PAIR), lambda p, s: (0, 0, p + first_pair)),
+                pl.BlockSpec((8, PAIR), lambda p, s: (0, p + first_pair)),
             ],
         ),
         out_shape=[
-            jax.ShapeDtypeStruct((count, pairs * 3 * PAIR), BF16),
-            jax.ShapeDtypeStruct((1, pairs * 3 * PAIR), F32),
+            jax.ShapeDtypeStruct((3, count, width), BF16),
+            jax.ShapeDtypeStruct((8, width), F32),
         ],
+        input_output_aliases={5: 0, 6: 1} if held else {},
         compiler_params=pltpu.CompilerParams(vmem_limit_bytes=VMEM),
-        cost_estimate=pl.CostEstimate(
-            flops=10 * count * 1024 * pairs * PAIR, bytes_accessed=20 * count * pairs * PAIR, transcendentals=count * 400 * 2 * pairs
-        ),
+        cost_estimate=QUICK,
         name="attention_backward",
-    )(starts, qkv, grad, att, stat)
+    )(starts, qkv, grad, att, stat, *held)
 
 
 ERF = (0.254829592, -0.284496736, 1.421413741, -1.453152027, 1.061405429)
@@ -289,107 +288,155 @@
     return u * phi, phi + u * bell * 0.3989422804014327
 
 
-def mlp_kernel(n, tile, chunk, *refs):
+def middle_kernel(n, tile, *refs):
     keep, rank, *pieces = refs[: n + 2]
-    (
-        att, xs, out_w, up_w, down_w, vectors, up_b,
-        result, middle_grad_out, att_low_out, normed_out, active_out, hidden_out, mlp_out, branch_out, att_grad_out,
-        sums, up_sums,
-    ) = refs[n + 2 :]
-    out_b, gain, shift, down_b = (vectors[i : i + 1, :] for i in range(4))
-    keep_attn, keep_mlp = keep[0], keep[1]
+    att, xs, out_w, vectors, cot_out, att_low_out, middle_out, normed_out, mlp_out, sums = refs[n + 2 :]
     step = pl.program_id(0)
     cot = sort_tile(rank[...], tile, step, pieces)
+    cot_out[...] = cot.astype(BF16)
+    mlp_grad = (cot * keep[1]).astype(BF16)
+    mlp_out[...] = mlp_grad
     att_low = att[...].astype(BF16)
     att_low_out[...] = att_low
-    middle = xs[...].astype(F32) + keep_attn * (dot(att_low, out_w[...]) + out_b)
-    hat, inv = centre_scale(middle)
-    normed = (hat * gain + shift).astype(BF16)
-    normed_out[...] = normed
-    mlp_grad = (cot * keep_mlp).astype(BF16)
-    mlp_out[...] = mlp_grad
+    middle = xs[...].astype(F32) + keep[0] * (dot(att_low, out_w[...]) + vectors[0:1, :])
+    middle_out[...] = middle
+    hat, _ = centre_scale(middle)
+    normed_out[...] = (hat * vectors[1:2, :] + vectors[2:3, :]).astype(BF16)
 
     @pl.when(step == 0)
     def _():
         sums[...] = jnp.zeros_like(sums)
-        up_sums[...] = jnp.zeros_like(up_sums)
-
-    lift = jnp.zeros(middle.shape, F32)
-    back = jnp.zeros(middle.shape, F32)
-    for c in range(up_w.shape[1] // chunk):
-        cols = slice(c * chunk, (c + 1) * chunk)
-        u = dot(normed, up_w[:, cols]) + up_b[:, cols]
-        act, slope = gelu_pair(u)
-        act = act.astype(BF16)
-        active_out[:, cols] = act
-        lift = lift + dot(act, down_w[cols, :])
-        hidden = (dot_nt(mlp_grad, down_w[cols, :]) * slope).astype(BF16)
-        hidden_out[:, cols] = hidden
-        up_sums[:, cols] += jnp.sum(hidden.astype(F32), axis=0, keepdims=True)
-        back = back + dot_nt(hidden, up_w[:, cols])
-    result[...] = (middle + keep_mlp * (lift + down_b)).astype(BF16)
-    middle_grad = cot + norm_back(back * gain, hat, inv)
-    middle_grad_out[...] = middle_grad
-    branch = (keep_attn * middle_grad).astype(BF16)
-    branch_out[...] = branch
-    att_grad_out[...] = dot_nt(branch, out_w[...]).astype(BF16)
-    sums[0:1, :] += jnp.sum(back * hat, axis=0, keepdims=True)
-    sums[1:2, :] += jnp.sum(back, axis=0, keepdims=True)
-    sums[2:3, :] += jnp.sum(mlp_grad.astype(F32), axis=0, keepdims=True)
-    sums[3:4, :] += jnp.sum(branch.astype(F32), axis=0, keepdims=True)
-
-
-def mlp_call(keep, rank, pieces, att, xs, out_w, up_w, down_w, vectors, up_b, tile=192, chunk=512):
+
+    sums[0:1, :] += jnp.sum(mlp_grad.astype(F32), axis=0, keepdims=True)
+
+
+def middle_call(keep, rank, pieces, att, xs, out_w, vectors, tile=384):
     n = len(pieces)
     span, width = pieces[0].shape
     count = n * span
-    ff = up_w.shape[1]
-
-    def rows(w):
-        return pl.BlockSpec((tile, w), lambda i: (i, 0))
-
-    def shape(w, dtype):
-        return jax.ShapeDtypeStruct((count, w), dtype)
-
+    rows = pl.BlockSpec((tile, width), lambda i: (i, 0))
+    low, full = jax.ShapeDtypeStruct((count, width), BF16), jax.ShapeDtypeStruct((count, width), F32)
     return pl.pallas_call(
-        functools.partial(mlp_kernel, n, tile, chunk),
+        functools.partial(middle_kernel, n, tile),
         grid=(count // tile,),
         in_specs=[pl.BlockSpec(memory_space=pltpu.SMEM), whole((1, count))]
         + [whole((span, width))] * n
-        + [rows(width), rows(width), whole(out_w.shape), whole(up_w.shape), whole(down_w.shape)]
-        + [whole(vectors.shape), whole(up_b.shape)],
-        out_specs=[rows(width)] * 4
-        + [rows(ff), rows(ff)]
-        + [rows(width)] * 3
-        + [pl.BlockSpec((8, width), lambda i: (0, 0)), pl.BlockSpec((1, ff), lambda i: (0, 0))],
-        out_shape=[
-            shape(width, BF16),
-            shape(width, F32),
-            shape(width, BF16),
-            shape(width, BF16),
-            shape(ff, BF16),
-            shape(ff, BF16),
-            shape(width, BF16),
-            shape(width, BF16),
-            shape(width, BF16),
-            jax.ShapeDtypeStruct((8, width), F32),
-            jax.ShapeDtypeStruct((1, ff), F32),
-        ],
+        + [rows, rows, whole(out_w.shape), whole(vectors.shape)],
+        out_specs=[rows] * 5 + [pl.BlockSpec((8, width), lambda i: (0, 0))],
+        out_shape=[low, low, full, low, low, jax.ShapeDtypeStruct((8, width), F32)],
         compiler_params=pltpu.CompilerParams(vmem_limit_bytes=VMEM),
-        cost_estimate=pl.CostEstimate(
-            flops=2 * count * width * (4 * ff + 2 * width), bytes_accessed=40 * count * width, transcendentals=2 * count * ff
+        cost_estimate=QUICK,
+        name="middle",
+    )(keep, rank, *pieces, att, xs, out_w, vectors)
+
+
+def mlp_kernel(parts, core, keep, normed, mlp_grad, middle, cot, out_w, vectors, up_w, up_b, down_w, *refs):
+    (
+        up_send, up_keep, down_send, down_keep, up_sums, result, middle_grad_out, branch_out, att_grad_out, sums,
+        lift, back, act_all, hidden_all,
+    ) = refs
+    step, steps = pl.program_id(0), pl.num_programs(0)
+    count = normed.shape[0]
+    cuts = [slice(i * (count // parts), (i + 1) * (count // parts)) for i in range(parts)]
+
+    @pl.when(step == 0)
+    def _():
+        lift[...] = jnp.zeros_like(lift)
+        back[...] = jnp.zeros_like(back)
+
+    total = jnp.zeros(up_sums.shape, F32)
+    for rows in cuts:
+        act, slope = gelu_pair(dot(normed[rows, :], up_w[...]) + up_b[...])
+        act = act.astype(BF16)
+        act_all[rows, :] = act
+        hidden = (dot_nt(mlp_grad[rows, :], down_w[...]) * slope).astype(BF16)
+        hidden_all[rows, :] = hidden
+        total = total + jnp.sum(hidden.astype(F32), axis=0, keepdims=True)
+        lift[rows, :] += dot(act, down_w[...])
+        back[rows, :] += dot_nt(hidden, up_w[...])
+    up_sums[...] = total
+    up_part = dot_tn(normed[...], hidden_all[...]).astype(BF16)
+    down_part = dot_tn(act_all[...], mlp_grad[...]).astype(BF16)
+
+    @pl.when(step < steps // 2)
+    def _():
+        up_send[...] = up_part
+        down_send[...] = down_part
+
+    @pl.when(step >= steps // 2)
+    def _():
+        up_keep[...] = up_part
+        down_keep[...] = down_part
+
+    @pl.when(step == steps - 1)
+    def _():
+        gain, down_b = vectors[1:2, :], vectors[3:4, :]
+        sums[...] = jnp.zeros_like(sums)
+        for rows in cuts:
+            mid, grad = middle[rows, :], back[rows, :]
+            hat, inv = centre_scale(mid)
+            result[rows, :] = (mid + keep[1] * (lift[rows, :] + down_b)).astype(BF16)
+            middle_grad = cot[rows, :].astype(F32) + norm_back(grad * gain, hat, inv)
+            middle_grad_out[rows, :] = middle_grad
+            branch = (keep[0] * middle_grad).astype(BF16)
+            branch_out[rows, :] = branch
+            att_grad_out[rows, :] = dot_nt(branch, out_w[...]).astype(BF16)
+            sums[0:1, :] += jnp.sum(grad * hat, axis=0, keepdims=True)
+            sums[1:2, :] += jnp.sum(grad, axis=0, keepdims=True)
+            sums[2:3, :] += jnp.sum(branch.astype(F32), axis=0, keepdims=True)
+
+
+def mlp_call(core, keep, normed, mlp_grad, middle, cot, out_w, vectors, up_w, up_b, down_w, chunk=512, parts=3):
+    count, width = normed.shape
+    ff = up_w.shape[1]
+    half = ff // 2 // chunk
+
+    def place(i, c):
+        return jnp.where(i < half, (1 - c[0]) * half + i, c[0] * half + i - half)
+
+    low, full = jax.ShapeDtypeStruct((count, width), BF16), jax.ShapeDtypeStruct((count, width), F32)
+    up_part, down_part = jax.ShapeDtypeStruct((width, ff // 2), BF16), jax.ShapeDtypeStruct((ff // 2, width), BF16)
+    return pl.pallas_call(
+        functools.partial(mlp_kernel, parts),
+        grid_spec=pltpu.PrefetchScalarGridSpec(
+            num_scalar_prefetch=1,
+            grid=(2 * half,),
+            in_specs=[
+                pl.BlockSpec(memory_space=pltpu.SMEM),
+                whole((count, width)),
+                whole((count, width)),
+                whole((count, width)),
+                whole((count, width)),
+                whole(out_w.shape),
+                whole(vectors.shape),
+                pl.BlockSpec((width, chunk), lambda i, c: (0, place(i, c))),
+                pl.BlockSpec((1, chunk), lambda i, c: (0, place(i, c))),
+                pl.BlockSpec((chunk, width), lambda i, c: (place(i, c), 0)),
+            ],
+            out_specs=[
+                pl.BlockSpec((width, chunk), lambda i, c: (0, jnp.minimum(i, half - 1))),
+                pl.BlockSpec((width, chunk), lambda i, c: (0, jnp.maximum(i - half, 0))),
+                pl.BlockSpec((chunk, width), lambda i, c: (jnp.minimum(i, half - 1), 0)),
+                pl.BlockSpec((chunk, width), lambda i, c: (jnp.maximum(i - half, 0), 0)),
+                pl.BlockSpec((1, chunk), lambda i, c: (0, place(i, c))),
+            ]
+            + [whole((count, width))] * 4
+            + [whole((8, width))],
+            scratch_shapes=[pltpu.VMEM((count, width), F32)] * 2 + [pltpu.VMEM((count, chunk), BF16)] * 2,
         ),
+        out_shape=[up_part, up_part, down_part, down_part, jax.ShapeDtypeStruct((1, ff), F32)]
+        + [low, full, low, low, jax.ShapeDtypeStruct((8, width), F32)],
+        compiler_params=pltpu.CompilerParams(vmem_limit_bytes=VMEM),
+        cost_estimate=QUICK,
         name="mlp",
-    )(keep, rank, *pieces, att, xs, out_w, up_w, down_w, vectors, up_b)
-
-
-def input_kernel(groups, *refs):
-    gs = refs[:groups]
-    weight, xs, middle_grad, gain, out, sums = refs[groups:]
-    span = gs[0].shape[1]
+    )(core, keep, normed, mlp_grad, middle, cot, out_w, vectors, up_w, up_b, down_w)
+
+
+def input_kernel(grads, weight, xs, middle_grad, gain, out, sums):
+    span = xs.shape[1]
     back = None
-    for i, g in enumerate(gs):
-        part = dot_nt(g[...], weight[:, i * span : (i + 1) * span])
+    for j in range(3):
+        part = dot_nt(grads[j], weight[:, j * span : (j + 1) * span])
         back = part if back is None else back + part
     hat, inv = centre_scale(xs[...].astype(F32))
     out[...] = (middle_grad[...] + norm_back(back * gain[...], hat, inv)).astype(BF16)
@@ -402,12 +449,12 @@
     sums[1:2, :] += jnp.sum(back, axis=0, keepdims=True)
 
 
-def input_call(gs, weight, xs, middle_grad, gain, tile=288):
+def input_call(grads, weight, xs, middle_grad, gain, tile=288):
     count, width = xs.shape
     return pl.pallas_call(
-        functools.partial(input_kernel, len(gs)),
+        input_kernel,
         grid=(count // tile,),
-        in_specs=[pl.BlockSpec((tile, g.shape[1]), lambda i: (i, 0)) for g in gs]
+        in_specs=[pl.BlockSpec((3, tile, width), lambda i: (0, i, 0))]
         + [
             whole(weight.shape),
             pl.BlockSpec((tile, width), lambda i: (i, 0)),
@@ -417,11 +464,9 @@
         out_specs=[pl.BlockSpec((tile, width), lambda i: (i, 0)), pl.BlockSpec((8, width), lambda i: (0, 0))],
         out_shape=[jax.ShapeDtypeStruct((count, width), BF16), jax.ShapeDtypeStruct((8, width), F32)],
         compiler_params=pltpu.CompilerParams(vmem_limit_bytes=VMEM),
-        cost_estimate=pl.CostEstimate(
-            flops=6 * count * width * width, bytes_accessed=16 * count * width, transcendentals=0
-        ),
+        cost_estimate=QUICK,
         name="input_backward",
-    )(*gs, weight, xs, middle_grad, gain)
+    )(grads, weight, xs, middle_grad, gain)
 
 
 def unsort_kernel(n, rank, xs, *outs):
@@ -440,11 +485,162 @@
         functools.partial(unsort_kernel, n),
         out_shape=[jax.ShapeDtypeStruct((span, width), BF16)] * n,
         compiler_params=pltpu.CompilerParams(vmem_limit_bytes=VMEM),
-        cost_estimate=pl.CostEstimate(
-            flops=2 * count * width * count, bytes_accessed=6 * count * width, transcendentals=0
-        ),
+        cost_estimate=QUICK,
         name="unsort",
     )(rank_col, xs)
+
+
+def weights_kernel(half, left, right, out):
+    out[...] = dot_tn(left[...], right[...]).astype(BF16)
+
+
+def weights_call(half, left, right, split_left, tile=768):
+    count, m = left.shape
+    n = right.shape[1]
+    tiles = (m if split_left else n) // 2 // tile
+
+    def cut(i, h):
+        return (0, h[0] * tiles + i)
+
+    if split_left:
+        specs = [pl.BlockSpec((count, tile), cut), whole((count, n))]
+        out, out_spec = (m // 2, n), pl.BlockSpec((tile, n), lambda i, h: (i, 0))
+    else:
+        specs = [whole((count, m)), pl.BlockSpec((count, tile), cut)]
+        out, out_spec = (m, n // 2), pl.BlockSpec((m, tile), lambda i, h: (0, i))
+    return pl.pallas_call(
+        weights_kernel,
+        grid_spec=pltpu.PrefetchScalarGridSpec(
+            num_scalar_prefetch=1, grid=(tiles,), in_specs=specs, out_specs=out_spec
+        ),
+        out_shape=jax.ShapeDtypeStruct(out, BF16),
+        compiler_params=pltpu.CompilerParams(vmem_limit_bytes=VMEM),
+        cost_estimate=QUICK,
+        name="weights",
+    )(half, left, right)
+
+
+def input_weights_kernel(half, normed, grads, *refs):
+    out, piece = refs[-1], normed[...]
+    span = grads.shape[2]
+    for j in range(3):
+        out[:, j * span : (j + 1) * span] = dot_tn(piece, grads[j]).astype(BF16)
+    if len(refs) == 3:
+        out[:, 3 * span :] = dot_tn(refs[0][...], refs[1][...]).astype(BF16)
+
+
+def input_weights_call(half, normed, grads, part, parts, *more):
+    count, width = normed.shape
+    span = width // parts
+    cols = 3 * span + (more[1].shape[1] if more else 0)
+    extra = [pl.BlockSpec((count, width // 2), lambda i, h: (0, h[0])), whole((count, width))] if more else []
+    return pl.pallas_call(
+        input_weights_kernel,
+        grid_spec=pltpu.PrefetchScalarGridSpec(
+            num_scalar_prefetch=1,
+            grid=(1,),
+            in_specs=[
+                pl.BlockSpec((count, width // 2), lambda i, h: (0, h[0])),
+                pl.BlockSpec((3, count, span), lambda i, h: (0, 0, part)),
+            ]
+            + extra,
+            out_specs=whole((width // 2, cols)),
+        ),
+        out_shape=jax.ShapeDtypeStruct((width // 2, cols), BF16),
+        compiler_params=pltpu.CompilerParams(vmem_limit_bytes=VMEM),
+        cost_estimate=QUICK,
+        name="input_weights",
+    )(half, normed, grads, *more)
+
+
+GROUP = 8
+
+
+def final_call(core, places, pairs, name, spread, outs):
+    groups = places.shape[0] // 2 - 1
+    n = len(pairs)
+
+    def kernel(c, t, *refs):
+        h = pl.program_id(0)
+        turn = t[2 * groups + h]
+
+        def write(sources):
+            blocks = [ref[...].astype(F32) for ref in sources]
+            rows = [block.shape[0] // GROUP for block in blocks]
+            for j in range(GROUP):
+                spread([b[j * r : (j + 1) * r] for b, r in zip(blocks, rows)], j ^ turn, refs[2 * n :])
+
+        pl.when(h == 0)(lambda: write(refs[:n]))
+        pl.when(h == 1)(lambda: write(refs[n : 2 * n]))
+
+    def in_spec(array, which):
+        rows = array.shape[0] // groups
+        if which == 0:
+            return pl.BlockSpec((rows, array.shape[1]), lambda h, s, c, t: (jnp.where(h == 0, s, groups - 1), 0))
+        return pl.BlockSpec((rows, array.shape[1]), lambda h, s, c, t: (jnp.where(h == 0, 0, s), 0))
+
+    def out_spec(block, index):
+        return pl.BlockSpec(block, lambda h, s, c, t: index(jnp.where(h == 0, c[0], 1 - c[0]), t[h * groups + s]))
+
+    return pl.pallas_call(
+        kernel,
+        grid_spec=pltpu.PrefetchScalarGridSpec(
+            num_scalar_prefetch=2,
+            grid=(2, groups),
+            in_specs=[in_spec(p[0], 0) for p in pairs] + [in_spec(p[1], 1) for p in pairs],
+            out_specs=[out_spec(block, index) for _, block, index in outs],
+        ),
+        out_shape=[jax.ShapeDtypeStruct(shape, F32) for shape, _, _ in outs],
+        compiler_params=pltpu.CompilerParams(vmem_limit_bytes=VMEM),
+        cost_estimate=QUICK,
+        name=name,
+    )(core, places, *[p[0] for p in pairs], *[p[1] for p in pairs])
+
+
+def rows_at(ref, place, value, *cols):
+    rows = value.shape[0]
+    ref[(pl.ds(pl.multiple_of(place * rows, 8), rows), *cols)] = value
+
+
+def down_final(core, places, held, other):
+    rows, cols = held.shape
+    groups = places.shape[0] // 2 - 1
+    block = (rows // groups, cols)
+
+    def spread(blocks, place, refs):
+        rows_at(refs[0], place, blocks[0], slice(None))
+
+    outs = [((2 * rows, cols), block, lambda h, t: (h * groups + t, 0))]
+    return final_call(core, places, [(held, other)], "down_final", spread, outs)[0]
+
+
+def up_final(core, places, held, other):
+    rows, cols = held.shape
+    groups = places.shape[0] // 2 - 1
+
+    def spread(blocks, place, refs):
+        rows_at(refs[0], place, blocks[0], slice(None))
+
+    outs = [((rows, 2 * cols), (rows // groups, cols), lambda h, t: (t, h))]
+    return final_call(core, places, [(held, other)], "up_final", spread, outs)[0]
+
+
+def input_final(core, places, pairs):
+    half = pairs[0][0].shape[0]
+    width = 2 * half
+    groups = places.shape[0] // 2 - 1
+    span = width // len(pairs)
+
+    def spread(blocks, place, refs):
+        for g, block in enumerate(blocks):
+            for j in range(3):
+                at = j * width + g * span
+                rows_at(refs[0], place, block[:, j * span : (j + 1) * span], slice(at, at + span))
+        rows_at(refs[1], place, blocks[0][:, 3 * span :], slice(None))
+
+    index = lambda h, t: (h * groups + t, 0)
+    outs = [((width, 3 * width), (half // groups, 3 * width), index), ((width, width), (half // groups, width), index)]
+    return final_call(core, places, pairs, "input_final", spread, outs)
 
 
 MICRO = 2
@@ -751,10 +947,6 @@
     return lax.optimization_barrier((value, *others))[0]
 
 
-def add_low(a, b):
-    return (a.astype(F32) + b.astype(F32)).astype(BF16)
-
-
 def axis_bits(axis):
     bits, bit = [], 1
     while bit < lax.axis_size(axis):
@@ -763,59 +955,119 @@
     return bits
 
 
-def scatter_sum(keep, recv, order):
-    for axis, bit in order:
-        half = keep.shape[0] // 2
-        own = side(axis, bit)
-
-        def part(which, keep=keep, recv=recv, half=half):
-            return add_low(
-                lax.dynamic_slice_in_dim(keep, which * half, half, 0),
-                lax.dynamic_slice_in_dim(recv, which * half, half, 0),
-            )
-
-        recv = swap(part(1 - own), axis, bit)
-        keep = part(own)
-    return add_low(keep, recv)
-
-
-def in_order(mine, other, own, dim):
-    mine, other = jnp.expand_dims(mine, dim), jnp.expand_dims(other, dim)
-    shape = [1] * mine.ndim
-    shape[dim] = 2
-    place = lax.broadcasted_iota(jnp.int32, shape, dim)
-    return jnp.where(place == own, mine, other)
-
-
-def gather_back(block, order):
-    for axis, bit in reversed(order):
-        pair = in_order(block, swap(block, axis, bit), side(axis, bit), 0)
-        block = pair.reshape(2 * block.shape[0], block.shape[1])
-    return block
-
-
-def sum_weights(make, orders, dim):
-    own = side("blk", 1)
-    send = make(1 - own)
-    recv = swap(send, "blk", 1)
-    keep = make(own)
-    cols = keep.shape[1] // len(orders)
-    parts = []
-    for i, order in enumerate(orders):
-        cut = slice(i * cols, (i + 1) * cols)
-        parts.append(gather_back(scatter_sum(keep[:, cut], recv[:, cut], order), order))
-    block = jnp.concatenate(parts, axis=1) if len(parts) > 1 else parts[0]
-    return in_order(block, swap(block, "blk", 1), own, dim).astype(F32)
-
-
-def sum_small(value):
-    for axis, bit in axis_bits("blk") + axis_bits("rows"):
-        value = value + swap(value, axis, bit)
-    return value
-
-
-def half_cols(array, which, size):
-    return lax.dynamic_slice_in_dim(array, which * size, size, 1)
+def add_low(a, b):
+    return (a.astype(F32) + b.astype(F32)).astype(BF16)
+
+
+def swap_two(value, step):
+    rows, blocks = lax.axis_size("rows"), lax.axis_size("blk")
+    pairs = []
+    for r in range(rows):
+        for b in range(blocks):
+            axis, bit = step[b % 2]
+            other = (r ^ bit, b) if axis == "rows" else (r, b ^ bit)
+            pairs.append((r * blocks + b, other[0] * blocks + other[1]))
+    return lax.ppermute(value, ("rows", "blk"), pairs)
+
+
+def side_two(step):
+    return jnp.where(side("blk", 1) == 0, side(*step[0]), side(*step[1]))
+
+
+class Order:
+    def __init__(self):
+        self.last = ()
+
+    def hold(self, value):
+        return after(value, *self.last) if self.last else value
+
+    def done(self, *values):
+        self.last = values
+        return values[0] if len(values) == 1 else values
+
+
+class Chain:
+    def __init__(self, order, steps):
+        self.order, self.steps, self.at = order, steps, 0
+
+    def start(self, make):
+        core = side("blk", 1).astype(jnp.int32).reshape(1)
+        self.begin(self.order.done(make(1 - core)), self.order.done(make(core)))
+
+    def begin(self, send, keep):
+        self.recv, self.keep = swap(send, "blk", 1), keep
+
+    def next(self, count=1):
+        for _ in range(count):
+            self._next()
+
+    def finish(self):
+        while not hasattr(self, "result"):
+            self._next()
+
+    def _next(self):
+        recv, keep, n = self.order.hold(self.recv), self.keep, len(self.steps)
+        if self.at < n:
+            step = self.steps[self.at]
+            half = keep.shape[0] // 2
+            own = side_two(step)
+
+            def part(which):
+                return add_low(
+                    lax.dynamic_slice_in_dim(keep, which * half, half, 0),
+                    lax.dynamic_slice_in_dim(recv, which * half, half, 0),
+                )
+
+            send, self.keep = part(1 - own), part(own)
+            self.recv = swap_two(send, step)
+        elif self.at <= 2 * n:
+            send = add_low(keep, recv) if self.at == n else jnp.concatenate([keep, recv], axis=0)
+            self.keep = send
+            back = 2 * n - 1 - self.at
+            self.recv = swap_two(send, self.steps[back]) if back >= 0 else swap(send, "blk", 1)
+        else:
+            self.result = (keep, recv)
+            return
+        self.at += 1
+        self.order.done(send, self.keep)
+
+
+def block_places(steps):
+    core = side("blk", 1)
+    bases = []
+    for c in range(2):
+        base = 0
+        for step in steps:
+            base = base * 2 + side(*step[c])
+        bases.append(base)
+    first = jnp.where(core == 0, bases[0], bases[1])
+    second = jnp.where(core == 0, bases[1], bases[0])
+    index = jnp.arange((1 << len(steps)) // GROUP, dtype=jnp.int32)
+    parts = [index ^ (first // GROUP), index ^ (second // GROUP), jnp.stack([first % GROUP, second % GROUP])]
+    return core.astype(jnp.int32).reshape(1), jnp.concatenate(parts).astype(jnp.int32)
+
+
+class Small:
+    def __init__(self, order, value):
+        self.order, self.value = order, value
+        self.steps = axis_bits("blk") + axis_bits("rows")
+        self.at = 0
+        self._send()
+
+    def _send(self):
+        if self.at < len(self.steps):
+            self.recv = swap(self.value, *self.steps[self.at])
+        self.at += 1
+
+    def next(self):
+        if self.at <= len(self.steps):
+            self.value = self.order.done(self.value + self.order.hold(self.recv))
+            self._send()
+
+    def finish(self):
+        while self.at <= len(self.steps):
+            self.next()
+        return self.value
 
 
 def local_rows(
@@ -843,10 +1095,13 @@
     def row_piece(array, s):
         return lax.dynamic_index_in_dim(array, me ^ s, 0, keepdims=False)
 
-    ids = [row_piece(image_index, 0)] + [swap(row_piece(image_index, s), "blk", s) for s in range(1, blocks)]
-    xs_in = [row_piece(inputs, 0)] + [swap(row_piece(inputs, s), "blk", s) for s in range(1, blocks)]
+    xs_send = [row_piece(inputs, s) for s in range(blocks)]
+    xs_in = xs_send[:1] + [swap(xs_send[s], "blk", s) for s in range(1, blocks)]
+    ids = [row_piece(image_index, 0)] + [
+        swap(row_piece(after(image_index, *xs_send), s), "blk", s) for s in range(1, blocks)
+    ]
     cots = [row_piece(cotangent, 0)] + [
-        swap(after(row_piece(cotangent, s), xs_in[-1]), "blk", s) for s in range(1, blocks)
+        swap(after(row_piece(cotangent, s), *xs_in), "blk", s) for s in range(1, blocks)
     ]
     ids = jnp.concatenate(ids)
     image = jnp.where(ids < 0, 4, ids)
@@ -857,64 +1112,103 @@
     keep = lax.dynamic_index_in_dim(keep_mask, me, 0, keepdims=False).astype(F32) / keep_rate
     rank_row, rank_col = rank[None, :], rank[:, None]
 
-    paired = input_weight.reshape(width, 3, PAIRS, PAIR).transpose(0, 2, 1, 3).reshape(width, 3 * width)
     bias = jnp.stack([input_bias[0], jnp.zeros_like(input_bias[0]), input_bias[1]])
-    bias = bias.reshape(3, PAIRS, PAIR).transpose(1, 0, 2).reshape(1, 3 * width)
-
-    xs, normed, qkv = qkv_call(rank_row, xs_in, first_gain[None], first_shift[None], paired, bias)
+    xs, normed, qkv = qkv_call(rank_row, xs_in, first_gain[None], first_shift[None], input_weight, bias)
     attended, stat = forward_call(starts, qkv)
     vectors = jnp.stack([output_bias, second_gain, second_shift, down_bias])
-    (result, middle_grad, att_low, normed2, active, hidden, mlp_grad, branch, att_grad, sums2, up_sums) = mlp_call(
-        keep, rank_row, cots, attended, xs, output_weight, up_weight, down_weight, vectors, up_bias[None]
+    core = side("blk", 1).astype(jnp.int32).reshape(1)
+    cot, att_low, middle, normed2, mlp_grad, sums_mid = middle_call(
+        keep, rank_row, cots, attended, xs, output_weight, vectors
+    )
+    (up_send, up_keep, down_send, down_keep, up_sums, result, middle_grad, branch, att_grad, sums2) = mlp_call(
+        core, keep, normed2, mlp_grad, middle, cot, output_weight, vectors, up_weight, up_bias[None], down_weight
     )
 
     y, x = axis_bits("blk")[1:], axis_bits("rows")[:1]
     z = axis_bits("rows")[1:]
-    low_z, high_z = z[:1], z[1:]
-    thirds = [x + low_z + y + high_z, low_z + x + y + high_z, y + x + low_z + high_z]
-    down_total = sum_weights(lambda h: dot_tn(half_cols(active, h, ff // 2), mlp_grad).astype(BF16), thirds, 0)
-    up_total = sum_weights(lambda h: dot_tn(normed2, half_cols(hidden, h, ff // 2)).astype(BF16), thirds, 1)
-    out_total = sum_weights(lambda h: dot_tn(att_low, half_cols(branch, h, width // 2)).astype(BF16), thirds[:1], 1)
-    small = sum_small(jnp.concatenate([sums2[:4], up_sums.reshape(4, width)]))
-
-    results = unsort_call(rank_col, result, blocks)
-    groups = 3
-    each = PAIRS // groups
-    grads, bias_sums, input_totals = [], [], []
-    for g in range(groups):
-        grad, col_sums = backward_call(starts, qkv, att_grad, attended, stat, g * each, each)
-        grads.append(grad)
-        bias_sums.append(col_sums)
-        total = sum_weights(
-            lambda h, grad=grad: dot_tn(normed, half_cols(grad, h, 3 * PAIR * each // 2)).astype(BF16), thirds[g : g + 1], 1
-        )
-        input_totals.append(total.reshape(width, each, 3, PAIR))
-    inputs_grad, sums1 = input_call(grads, paired, xs, middle_grad, first_gain[None])
-    back = unsort_call(rank_col, inputs_grad, blocks)
-    bias_sum = jnp.concatenate(bias_sums, axis=1).reshape(PAIRS, 3, PAIR).transpose(1, 0, 2).reshape(3, width)
-    small_last = sum_small(jnp.concatenate([sums1[:2], bias_sum]))
-    input_total = jnp.concatenate(input_totals, axis=1).transpose(0, 2, 1, 3).reshape(width, 3 * width)
-
-    def send_back(pieces):
-        home = [pieces[0]] + [swap(pieces[s], "blk", s) for s in range(1, blocks)]
-        stacked = jnp.stack(home)
+    low_z, rest = z[:1], z[1:]
+
+    def steps(first, second):
+        return list(zip(first + rest, second + rest))
+
+    xy = steps(x + y + low_z, y + x + low_z)
+    zx = steps(low_z + y + x, x + low_z + y)
+    yz = steps(y + low_z + x, low_z + y + x)
+    order = Order()
+    order.done(att_grad)
+
+    def send_home(pieces):
+        return [pieces[0]] + [swap(pieces[s], "blk", s) for s in range(1, blocks)]
+
+    def at_home(pieces):
+        stacked = jnp.stack(pieces)
         return jnp.stack([lax.dynamic_index_in_dim(stacked, me ^ r, 0, keepdims=False) for r in range(blocks)])
 
+    down, up, first_in, last_in = Chain(order, xy), Chain(order, zx), Chain(order, yz), Chain(order, yz)
+    down.begin(down_send, down_keep)
+    up.begin(up_send, up_keep)
+    results = send_home(order.done(*unsort_call(rank_col, order.hold(result), blocks)))
+    rounds = 2 * len(xy) + 2
+
+    def advance(*chains):
+        for chain in chains:
+            if chain.at < rounds - 1:
+                chain.next()
+
+    advance(down, up)
+    parts = 2
+    each = PAIRS // parts
+    first = backward_call(starts, qkv, order.hold(att_grad), attended, stat, 0, each)
+    order.done(first[0])
+    advance(down, up)
+    first_in.start(lambda h: input_weights_call(h, order.hold(normed), first[0], 0, parts, att_low, branch))
+    advance(down, up)
+    grads, bias_sums = backward_call(starts, qkv, order.hold(att_grad), attended, stat, each, each, first)
+    order.done(grads)
+    advance(first_in, down, up)
+    last_in.start(lambda h: input_weights_call(h, order.hold(normed), grads, 1, parts))
+    advance(first_in, down, up)
+    inputs_grad, sums1 = order.done(*input_call(grads, input_weight, xs, order.hold(middle_grad), first_gain[None]))
+    small = Small(
+        order,
+        jnp.concatenate([sums1[:2], bias_sums[:3], sums2[:3], sums_mid[:1], up_sums.reshape(ff // width, width)]),
+    )
+    advance(last_in, first_in, down, up)
+    home = send_home(order.done(*unsort_call(rank_col, order.hold(inputs_grad), blocks)))
+    for _ in range(3):
+        advance(last_in, first_in, down, up)
+        small.next()
+    advance(last_in, first_in)
+    small.next()
+    down.finish()
+    down_total = order.done(down_final(*block_places(xy), *down.result))
+    advance(last_in, first_in)
+    small.next()
+    up.finish()
+    up_total = order.done(up_final(*block_places(zx), *up.result))
+    while last_in.at < rounds - 1 or first_in.at < rounds - 1:
+        advance(last_in, first_in)
+        small.next()
+    sums = small.finish()
+    first_in.finish()
+    last_in.finish()
+    input_total, out_total = input_final(*block_places(yz), [first_in.result, last_in.result])
+
     return (
-        send_back(results),
-        send_back(back),
-        small_last[0],
-        small_last[1],
+        at_home(results),
+        at_home(home),
+        sums[0],
+        sums[1],
         input_total,
-        jnp.stack([small_last[2], small_last[4]]),
-        out_total.reshape(width, width),
-        small[3],
-        small[0],
-        small[1],
-        up_total.reshape(width, ff),
-        small[4:].reshape(ff),
-        down_total.reshape(ff, width),
-        small[2],
+        jnp.stack([sums[2], sums[4]]),
+        out_total,
+        sums[7],
+        sums[5],
+        sums[6],
+        up_total,
+        sums[9:].reshape(ff),
+        down_total,
+        sums[8],
     )
 
 

time: 602 us -> 444 us (0.74)
  local copies, waits for them, and re-layouts: 87.4 us -> 26.6 us
  Pallas kernels: 158 us -> 208 us
  starting transfers between devices: 115 us -> 67.8 us
  waiting for transfers between devices: 121 us -> 79.7 us
  matrix products: 40.7 us -> 0 us
  other arithmetic: 68.9 us -> 52 us
    ppermute x117 -> x28, waiting for transfers between devices: 121 us -> 28.2 us  [swap(): lax.ppermute(value, axis, [(i, i ^ bit) for i in range(lax.axis_size(axis...]
    ppermute x117 -> x28, starting transfers between devices: 115 us -> 31.7 us  [swap(): lax.ppermute(value, axis, [(i, i ^ bit) for i in range(lax.axis_size(axis...]
    pallas_call x2 -> x10, Pallas kernels: 71.2 us -> 126 us  [the longest x1 59 us: mlp_call(): pl.pallas_call(functools.partial(mlp_kernel, parts), grid_spec=pltpu.Pref...]
    ppermute x0 -> x32, waiting for transfers between devices: none -> 51.5 us  [swap_two(): return lax.ppermute(value, ('rows', 'blk'), pairs)]
    dot_general x12 -> x0, matrix products: 40.7 us -> none  [dot_tn(): lax.dot_general(a, b, (((0,), (0,)), ((), ())), preferred_element_type=F32)]
    ppermute x0 -> x32, starting transfers between devices: none -> 36.2 us  [swap_two(): return lax.ppermute(value, ('rows', 'blk'), pairs)]
    select_n x28 -> x0, other arithmetic: 33.8 us -> none  [in_order(): return jnp.where(place == own, mine, other)]
    broadcast_in_dim x48 -> x0, local copies, waits for them, and re-layouts: 27.3 us -> none  [in_order(): return jnp.where(place == own, mine, other)]
  transfers between devices with their start and end apart: 117 -> 60, of which waited for: 40 -> 14; matrix products, arithmetic and copies ran while one was open for 25% -> 16% of each run, Pallas kernels for 9% -> 28%
where the time goes in v2:
time: 444 us; the launch traced here: 436 us
  Pallas kernels  208 us (47%)
  waiting for transfers between devices  79.7 us (18%)
  starting transfers between devices  67.8 us (15%)
  other arithmetic  52 us (12%)
  local copies, waits for them, and re-layouts  26.6 us (6%)
    pallas_call x1, Pallas kernels, mlp_call(): pl.pallas_call(functools.partial(mlp_kernel, parts), grid_spec=pltpu.Pref...  59 us
    ppermute x32, waiting for transfers between devices, swap_two(): return lax.ppermute(value, ('rows', 'blk'), pairs)  51.5 us
    pallas_call x2, Pallas kernels, backward_call(): pl.pallas_call(backward_kernel, grid_spec=pltpu.PrefetchScalarGridSpec(nu...  38.8 us
    ppermute x32, starting transfers between devices, swap_two(): return lax.ppermute(value, ('rows', 'blk'), pairs)  36.2 us
    ppermute x28, starting transfers between devices, swap(): lax.ppermute(value, axis, [(i, i ^ bit) for i in range(lax.axis_size(axis...  31.7 us
    ppermute x28, waiting for transfers between devices, swap(): lax.ppermute(value, axis, [(i, i ^ bit) for i in range(lax.axis_size(axis...  28.2 us
    convert_element_type x16, other arithmetic, add_low(): return (a.astype(F32) + b.astype(F32)).astype(BF16)  27.1 us
    pallas_call x3, Pallas kernels, final_call(): pl.pallas_call(kernel, grid_spec=pltpu.PrefetchScalarGridSpec(num_scalar_...  22.9 us
  transfers between devices with their start and end apart: 60, of which 14 were waited for; matrix products, arithmetic and copies ran while one was open for 16% of the time, Pallas kernels for 28%

profile of v2, /device:TPU:0, one launch (start us, length us, event | category | flops | bytes accessed | tf_op | source)
XLA Modules:
  0.0 436.3 jit_solution(3939576023731628329)
XLA Ops:
  13.0 13.5 %collective-permute-done.1 = s32[288]{0:T(512)S(1)} collective-permute-done((s32[288]{0:T(512)S(1)}, s32[288]{0:T(512)S(1)}, u32[]{:S(2)}, u32[]{:S(2)}) %collective-permute-start.1) | collective-permute-done | bytes 1184 | tf_op jit(solution)/shard_map/ppermute | solution.py:939
  30.5 16.3 %sort_qkv.1 = (bf16[1152,768]{1,0:T(8,128)(2,1)}, bf16[1152,768]{1,0:T(8,128)(2,1)}, bf16[3,1152,768]{2,1,0:T(8,128)(2,1)}) custom-call(s32[1,1152]{1,0:T(1,128)} %broadcast_in_dim.26.refs_0_.refs_1_, bf16[288,768]{1,0:T(8,128)(2,1)} %get-tuple-element.247.refs_1_, bf16[288,768]{1,0:T(8,128)(2,1)} %copy-done.12, bf16[288,768]{1,0:T(8,128)(2,1)} %copy-done.13, ...), custom_call_target="tpu_custom_call" | custom-call | flops 1048576 | bytes 65536 | tf_op jit(solution)/shard_map/sort_qkv/pallas_call | solution.py:82
  46.8 17.9 %attention_forward.1 = (f32[1152,768]{1,0:T(8,128)}, f32[1152,768]{1,0:T(8,128)}) custom-call(s32[6]{0:T(128)} %convert_reduce_fusion.1.starts, bf16[3,1152,768]{2,1,0:T(8,128)(2,1)} %get-tuple-element.113.qkv), custom_call_target="tpu_custom_call" | custom-call | flops 1048576 | bytes 65536 | tf_op jit(solution)/shard_map/attention_forward/pallas_call | solution.py:157
  64.7 11.3 %middle.1 = (bf16[1152,768]{1,0:T(8,128)(2,1)}, bf16[1152,768]{1,0:T(8,128)(2,1)}, f32[1152,768]{1,0:T(8,128)}, bf16[1152,768]{1,0:T(8,128)(2,1)}, bf16[1152,768]{1,0:T(8,128)(2,1)}, /*index=5*/f32[8,768]{1,0:T(8,128)}) custom-call(f32[2]{0:T(128)} %fusion.6.refs_0_.keep, s32[1,1152]{1,0:T(1,128)} %broadcast_in_dim.26.refs_0_.refs_1_, ...), custom_call_target="tpu_custom_call" | custom-call | flops 1048576 | bytes 65536 | tf_op jit(solution)/shard_map/middle/pallas_call | solution.py:319
  76.0 59.0 %mlp.1 = (bf16[768,1536]{1,0:T(8,128)(2,1)}, bf16[768,1536]{1,0:T(8,128)(2,1)}, bf16[1536,768]{1,0:T(8,128)(2,1)}, bf16[1536,768]{1,0:T(8,128)(2,1)}, f32[1,3072...) custom-call(s32[1]{0:T(128)} %bitcast.4.core.half.c, ...), custom_call_target="tpu_custom_call" | custom-call | flops 1048576 | bytes 65536 | tf_op jit(solution)/shard_map/mlp/pallas_call | solution.py:399
  136.6 5.0 %unsort.2 = (bf16[288,768]{1,0:T(8,128)(2,1)}, bf16[288,768]{1,0:T(8,128)(2,1)}, bf16[288,768]{1,0:T(8,128)(2,1)}, bf16[288,768]{1,0:T(8,128)(2,1)}) custom-call(s32[1152,1]{1,0:T(8,128)} %broadcast_in_dim.30.rank, bf16[1152,768]{1,0:T(8,128)(2,1)} %get-tuple-element.122.xs), custom_call_target="tpu_custom_call" | custom-call | flops 1048576 | bytes 65536 | tf_op jit(solution)/shard_map/unsort/pallas_call | solution.py:484
  141.6 4.1 add_convert_fusion.2
  147.3 3.6 add_convert_fusion.1
  152.7 19.3 %attention_backward.2 = (bf16[3,1152,768]{2,1,0:T(8,128)(2,1)}, f32[8,768]{1,0:T(8,128)}) custom-call(s32[6]{0:T(128)} %convert_reduce_fusion.1.starts, bf16[3,1152,768]{2,1,0:T(8,128)(2,1)} %get-tuple-element.113.qkv, bf16[1152,768]{1,0:T(8,128)(2,1)} %get-tuple-element.145.grad, f32[1152,768]{1,0:T(8,128)} %get-tuple-element.114.refs_6_.att, ...), custom_call_target="tpu_custom_call" | custom-call | flops 1048576 | bytes 65536 | tf_op jit(solution)/shard_map/attention_backward/pallas_call | solution.py:252
  176.9 6.3 %input_weights.4 = bf16[384,1920]{1,0:T(8,128)(2,1)} custom-call(s32[1]{0:T(128)S(6)} %sub.146.half, bf16[1152,768]{1,0:T(8,128)(2,1)} %get-tuple-element.153.normed, bf16[3,1152,768]{2,1,0:T(8,128)(2,1)} %get-tuple-element.135.grads.refs_0_, bf16[1152,768]{1,0:T(8,128)(2,1)} %get-tuple-element.140.refs_0_, bf16[1152,768]{1,0:T(8,128)(2,1)} %get-tuple-element.141.refs_1_), custom_call_target="tpu_custom_call" | custom-call | flops 1048576 | bytes 65536 | tf_op jit(solution)/shard_map/input_weights/pallas_call | solution.py:537
  185.4 6.3 %input_weights.5 = bf16[384,1920]{1,0:T(8,128)(2,1)} custom-call(s32[1]{0:T(128)} %bitcast.4.core.half.c, bf16[1152,768]{1,0:T(8,128)(2,1)} %get-tuple-element.153.normed, bf16[3,1152,768]{2,1,0:T(8,128)(2,1)} %get-tuple-element.135.grads.refs_0_, bf16[1152,768]{1,0:T(8,128)(2,1)} %get-tuple-element.140.refs_0_, bf16[1152,768]{1,0:T(8,128)(2,1)} %get-tuple-element.141.refs_1_), custom_call_target="tpu_custom_call" | custom-call | flops 1048576 | bytes 65536 | tf_op jit(solution)/shard_map/input_weights/pallas_call | solution.py:537
  195.6 4.2 collective-permute-done.16
  200.7 19.5 %attention_backward.3 = (bf16[3,1152,768]{2,1,0:T(8,128)(2,1)}, f32[8,768]{1,0:T(8,128)}) custom-call(s32[6]{0:T(128)} %convert_reduce_fusion.1.starts, bf16[3,1152,768]{2,1,0:T(8,128)(2,1)} %get-tuple-element.113.qkv, bf16[1152,768]{1,0:T(8,128)(2,1)} %get-tuple-element.145.grad, ...), custom_call_target="tpu_custom_call", output_to_operand_aliasing={{0}: (5, {}), {1}: (6, {})} | custom-call | flops 1048576 | bytes 65536 | tf_op jit(solution)/shard_map/attention_backward/pallas_call | solution.py:252
  220.2 2.9 add_convert_fusion.4
  229.9 4.9 %collective-permute-done.19 = bf16[192,768]{1,0:T(8,128)(2,1)S(1)} collective-permute-done((bf16[192,768]{1,0:T(8,128)(2,1)S(1)}, bf16[192,768]{1,0:T(8,128)(2,1)S(1)}, u32[]{:S(2)}, u32[]{:S(2)}) %collective-permute-start.19) | collective-permute-done | bytes 294944 | tf_op jit(solution)/shard_map/ppermute | solution.py:970
  239.3 4.6 %input_weights.6 = bf16[384,1152]{1,0:T(8,128)(2,1)} custom-call(s32[1]{0:T(128)S(6)} %sub.146.half, bf16[1152,768]{1,0:T(8,128)(2,1)} %get-tuple-element.153.normed, bf16[3,1152,768]{2,1,0:T(8,128)(2,1)} %get-tuple-element.147.grads), custom_call_target="tpu_custom_call" | custom-call | flops 1048576 | bytes 65536 | tf_op jit(solution)/shard_map/input_weights/pallas_call | solution.py:537
  243.9 4.7 %input_weights.7 = bf16[384,1152]{1,0:T(8,128)(2,1)} custom-call(s32[1]{0:T(128)} %bitcast.4.core.half.c, bf16[1152,768]{1,0:T(8,128)(2,1)} %get-tuple-element.153.normed, bf16[3,1152,768]{2,1,0:T(8,128)(2,1)} %get-tuple-element.147.grads), custom_call_target="tpu_custom_call" | custom-call | flops 1048576 | bytes 65536 | tf_op jit(solution)/shard_map/input_weights/pallas_call | solution.py:537
  256.3 10.4 %input_backward.1 = (bf16[1152,768]{1,0:T(8,128)(2,1)}, f32[8,768]{1,0:T(8,128)}) custom-call(bf16[3,1152,768]{2,1,0:T(8,128)(2,1)} %get-tuple-element.147.grads, bf16[768,2304]{1,0:T(8,128)(2,1)} %weight.1, bf16[1152,768]{1,0:T(8,128)(2,1)} %get-tuple-element.115.refs_7_.xs, f32[1152,768]{1,0:T(8,128)} %get-tuple-element.157.middle_grad, ...), custom_call_target="tpu_custom_call" | custom-call | flops 1048576 | bytes 65536 | tf_op jit(solution)/shard_map/input_backward/pallas_call | solution.py:454
  277.1 4.9 %unsort.3 = (bf16[288,768]{1,0:T(8,128)(2,1)}, bf16[288,768]{1,0:T(8,128)(2,1)}, bf16[288,768]{1,0:T(8,128)(2,1)}, bf16[288,768]{1,0:T(8,128)(2,1)}) custom-call(s32[1152,1]{1,0:T(8,128)} %broadcast_in_dim.30.rank, bf16[1152,768]{1,0:T(8,128)(2,1)} %get-tuple-element.164.xs), custom_call_target="tpu_custom_call" | custom-call | flops 1048576 | bytes 65536 | tf_op jit(solution)/shard_map/unsort/pallas_call | solution.py:484
  292.3 6.2 %collective-permute-done.38 = bf16[384,768]{1,0:T(8,128)(2,1)S(1)} collective-permute-done((bf16[384,768]{1,0:T(8,128)(2,1)S(1)}, bf16[384,768]{1,0:T(8,128)(2,1)S(1)}, u32[]{:S(2)}, u32[]{:S(2)}) %collective-permute-start.38) | collective-permute-done | bytes 589856 | tf_op jit(solution)/shard_map/ppermute | solution.py:970
  303.0 7.7 %collective-permute-done.37 = bf16[192,1536]{1,0:T(8,128)(2,1)S(1)} collective-permute-done((bf16[192,1536]{1,0:T(8,128)(2,1)S(1)}, bf16[192,1536]{1,0:T(8,128)(2,1)S(1)}, u32[]{:S(2)}, u32[]{:S(2)}) %collective-permute-start.37) | collective-permute-done | bytes 589856 | tf_op jit(solution)/shard_map/ppermute | solution.py:970
  311.7 17.7 %collective-permute-done.45 = bf16[48,1152]{1,0:T(8,128)(2,1)S(1)} collective-permute-done((bf16[48,1152]{1,0:T(8,128)(2,1)S(1)}, bf16[48,1152]{1,0:T(8,128)(2,1)S(1)}, u32[]{:S(2)}, u32[]{:S(2)}) %collective-permute-start.45) | collective-permute-done | bytes 110624 | tf_op jit(solution)/shard_map/ppermute | solution.py:970
  341.0 5.5 %collective-permute-done.10 = bf16[288,768]{1,0:T(8,128)(2,1)S(1)} collective-permute-done((bf16[288,768]{1,0:T(8,128)(2,1)}, bf16[288,768]{1,0:T(8,128)(2,1)S(1)}, u32[]{:S(2)}, u32[]{:S(2)}) %collective-permute-start.10) | collective-permute-done | bytes 442400 | tf_op jit(solution)/shard_map/ppermute | solution.py:939
  346.6 7.4 %collective-permute-done.11 = bf16[288,768]{1,0:T(8,128)(2,1)S(1)} collective-permute-done((bf16[288,768]{1,0:T(8,128)(2,1)}, bf16[288,768]{1,0:T(8,128)(2,1)S(1)}, u32[]{:S(2)}, u32[]{:S(2)}) %collective-permute-start.11) | collective-permute-done | bytes 442400 | tf_op jit(solution)/shard_map/ppermute | solution.py:939
  358.5 5.2 %collective-permute-done.47 = bf16[48,1920]{1,0:T(8,128)(2,1)S(1)} collective-permute-done((bf16[48,1920]{1,0:T(8,128)(2,1)S(1)}, bf16[48,1920]{1,0:T(8,128)(2,1)S(1)}, u32[]{:S(2)}, u32[]{:S(2)}) %collective-permute-start.47) | collective-permute-done | bytes 184352 | tf_op jit(solution)/shard_map/ppermute | solution.py:970
  366.8 7.9 %down_final.1 = f32[3072,768]{1,0:T(8,128)} custom-call(s32[1]{0:T(128)} %bitcast.4.core.half.c, s32[6]{0:T(128)} %pad_add_fusion.t, bf16[1536,768]{1,0:T(8,128)(2,1)} %constant_dynamic-update-slice_fusion.refs_0_, bf16[1536,768]{1,0:T(8,128)(2,1)} %collective-permute-done.52.refs_1_), custom_call_target="tpu_custom_call" | custom-call | flops 1048576 | bytes 65536 | tf_op jit(solution)/shard_map/down_final/pallas_call | solution.py:585
  385.9 4.5 %collective-permute-start.30 = (bf16[288,768]{1,0:T(8,128)(2,1)}, bf16[288,768]{1,0:T(8,128)(2,1)}, u32[]{:S(2)}, u32[]{:S(2)}) collective-permute-start(bf16[288,768]{1,0:T(8,128)(2,1)} %get-tuple-element.168), channel_id=1, source_target_pairs={{0,3},{1,2},{2,1},{3,0},{4,7},{5,6},{6,5},{7,4},{8,11},{9,10},{10,... | collective-permute-start | bytes 1327112 | tf_op jit(solution)/shard_map/ppermute | solution.py:939
  390.5 7.6 %up_final.1 = f32[768,3072]{1,0:T(8,128)} custom-call(s32[1]{0:T(128)} %bitcast.4.core.half.c, s32[6]{0:T(128)} %pad_add_fusion.2.t, bf16[768,1536]{1,0:T(8,128)(2,1)} %constant_dynamic-update-slice_fusion.5.refs_0_, bf16[768,1536]{1,0:T(8,128)(2,1)} %collective-permute-done.55.refs_1_), custom_call_target="tpu_custom_call" | custom-call | flops 1048576 | bytes 65536 | tf_op jit(solution)/shard_map/up_final/pallas_call | solution.py:585
  402.0 2.9 collective-permute-done.56
  407.7 7.6 %collective-permute-start.58 = (bf16[384,1920]{1,0:T(8,128)(2,1)}, bf16[384,1920]{1,0:T(8,128)(2,1)}, u32[]{:S(2)}, u32[]{:S(2)}) collective-permute-start(bf16[384,1920]{1,0:T(8,128)(2,1)} %constant_dynamic-update-slice_fusion.10.refs_0_), channel_id=1, source_target_pairs={{0,1},{1,0},{2,3},{3,2},{4,5},{5,4},{6,7},{7,6},{8,9},{9,8},{10,11... | collective-permute-start | bytes 4423688 | tf_op jit(solution)/shard_map/ppermute | solution.py:939
  416.8 4.9 %collective-permute-start.59 = (bf16[384,1152]{1,0:T(8,128)(2,1)}, bf16[384,1152]{1,0:T(8,128)(2,1)}, u32[]{:S(2)}, u32[]{:S(2)}) collective-permute-start(bf16[384,1152]{1,0:T(8,128)(2,1)} %constant_dynamic-update-slice_fusion.15.refs_1_), channel_id=1, source_target_pairs={{0,1},{1,0},{2,3},{3,2},{4,5},{5,4},{6,7},{7,6},{8,9},{9,8},{10,11... | collective-permute-start | bytes 2654216 | tf_op jit(solution)/shard_map/ppermute | solution.py:939
  428.3 7.5 %input_final.1 = (f32[768,2304]{1,0:T(8,128)}, f32[768,768]{1,0:T(8,128)}) custom-call(s32[1]{0:T(128)} %bitcast.4.core.half.c, s32[6]{0:T(128)} %pad_add_fusion.1.t, bf16[384,1920]{1,0:T(8,128)(2,1)} %constant_dynamic-update-slice_fusion.10.refs_0_, bf16[384,1152]{1,0:T(8,128)(2,1)} %constant_dynamic-update-slice_fusion.15.refs_1_, ...), custom_call_target="tpu_custom_call" | custom-call | flops 1048576 | bytes 65536 | tf_op jit(solution)/shard_map/input_final/pallas_call | solution.py:585
  (273 shorter events, 123.3 us)
Async XLA Ops:
  3.1 23.4 %collective-permute-start.3 = (bf16[288,768]{1,0:T(8,128)(2,1)S(1)}, bf16[288,768]{1,0:T(8,128)(2,1)S(1)}, u32[]{:S(2)}, u32[]{:S(2)}) collective-permute-start(bf16[288,768]{1,0:T(8,128)(2,1)S(1)} %get-tuple-element.246), channel_id=1, source_target_pairs={{0,1},{1,0},{2,3},{3,2},{4,5},{5,4},{6,7},{7,6},{8,9},{9,8},{10,11... | collective-permute-start | bytes 1327112 | tf_op jit(solution)/shard_map/ppermute | solution.py:939
  3.6 23.0 %collective-permute-start.4 = (bf16[288,768]{1,0:T(8,128)(2,1)S(1)}, bf16[288,768]{1,0:T(8,128)(2,1)S(1)}, u32[]{:S(2)}, u32[]{:S(2)}) collective-permute-start(bf16[288,768]{1,0:T(8,128)(2,1)S(1)} %get-tuple-element.248), channel_id=1, source_target_pairs={{0,2},{1,3},{2,0},{3,1},{4,6},{5,7},{6,4},{7,5},{8,10},{9,11},{10,... | collective-permute-start | bytes 1327112 | tf_op jit(solution)/shard_map/ppermute | solution.py:939
  6.1 20.5 %collective-permute-start.5 = (bf16[288,768]{1,0:T(8,128)(2,1)S(1)}, bf16[288,768]{1,0:T(8,128)(2,1)S(1)}, u32[]{:S(2)}, u32[]{:S(2)}) collective-permute-start(bf16[288,768]{1,0:T(8,128)(2,1)S(1)} %get-tuple-element.245), channel_id=1, source_target_pairs={{0,3},{1,2},{2,1},{3,0},{4,7},{5,6},{6,5},{7,4},{8,11},{9,10},{10,... | collective-permute-start | bytes 1327112 | tf_op jit(solution)/shard_map/ppermute | solution.py:939
  6.4 20.1 %collective-permute-start.1 = (s32[288]{0:T(512)S(1)}, s32[288]{0:T(512)S(1)}, u32[]{:S(2)}, u32[]{:S(2)}) collective-permute-start(s32[288]{0:T(512)S(1)} %get-tuple-element.211), channel_id=1, source_target_pairs={{0,2},{1,3},{2,0},{3,1},{4,6},{5,7},{6,4},{7,5},{8,10},{9,11},{10,... | collective-permute-start | bytes 3464 | tf_op jit(solution)/shard_map/ppermute | solution.py:939
  26.6 38.1 %collective-permute-start.6 = (bf16[288,768]{1,0:T(8,128)(2,1)}, bf16[288,768]{1,0:T(8,128)(2,1)}, u32[]{:S(2)}, u32[]{:S(2)}) collective-permute-start(bf16[288,768]{1,0:T(8,128)(2,1)} %get-tuple-element.110), channel_id=1, source_target_pairs={{0,1},{1,0},{2,3},{3,2},{4,5},{5,4},{6,7},{7,6},{8,9},{9,8},{10,11... | collective-permute-start | bytes 1327112 | tf_op jit(solution)/shard_map/ppermute | solution.py:939
  26.8 37.9 %collective-permute-start.7 = (bf16[288,768]{1,0:T(8,128)(2,1)}, bf16[288,768]{1,0:T(8,128)(2,1)}, u32[]{:S(2)}, u32[]{:S(2)}) collective-permute-start(bf16[288,768]{1,0:T(8,128)(2,1)} %get-tuple-element.111), channel_id=1, source_target_pairs={{0,2},{1,3},{2,0},{3,1},{4,6},{5,7},{6,4},{7,5},{8,10},{9,11},{10,... | collective-permute-start | bytes 1327112 | tf_op jit(solution)/shard_map/ppermute | solution.py:939
  28.5 36.2 %collective-permute-start.8 = (bf16[288,768]{1,0:T(8,128)(2,1)S(1)}, bf16[288,768]{1,0:T(8,128)(2,1)}, u32[]{:S(2)}, u32[]{:S(2)}) collective-permute-start(bf16[288,768]{1,0:T(8,128)(2,1)S(1)} %get-tuple-element.112), channel_id=1, source_target_pairs={{0,3},{1,2},{2,1},{3,0},{4,7},{5,6},{6,5},{7,4},{8,11},{9,10},{10,... | collective-permute-start | bytes 1327112 | tf_op jit(solution)/shard_map/ppermute | solution.py:939
  145.7 26.3 %collective-permute-start.15 = (bf16[768,768]{1,0:T(8,128)(2,1)}, bf16[768,768]{1,0:T(8,128)(2,1)}, u32[]{:S(2)}, u32[]{:S(2)}) collective-permute-start(bf16[768,768]{1,0:T(8,128)(2,1)} %get-tuple-element.224), channel_id=1, source_target_pairs={{0,4},{1,3},{2,6},{3,1},{4,0},{5,7},{6,2},{7,5},{8,12},{9,11},{10,... | collective-permute-start | bytes 3538952 | tf_op jit(solution)/shard_map/ppermute | solution.py:970
  150.9 23.5 %collective-permute-start.14 = (bf16[384,1536]{1,0:T(8,128)(2,1)}, bf16[384,1536]{1,0:T(8,128)(2,1)}, u32[]{:S(2)}, u32[]{:S(2)}) collective-permute-start(bf16[384,1536]{1,0:T(8,128)(2,1)} %get-tuple-element.222), channel_id=1, source_target_pairs={{0,8},{1,5},{2,10},{3,7},{4,12},{5,1},{6,14},{7,3},{8,0},{9,13},{1... | collective-permute-start | bytes 3538952 | tf_op jit(solution)/shard_map/ppermute | solution.py:970
  183.2 36.9 %collective-permute-start.20 = (bf16[384,1920]{1,0:T(8,128)(2,1)}, bf16[384,1920]{1,0:T(8,128)(2,1)}, u32[]{:S(2)}, u32[]{:S(2)}) collective-permute-start(bf16[384,1920]{1,0:T(8,128)(2,1)} %input_weights.4), channel_id=1, source_target_pairs={{0,1},{1,0},{2,3},{3,2},{4,5},{5,4},{6,7},{7,6},{8,9},{9,8},{10,11... | collective-permute-start | bytes 4423688 | tf_op jit(solution)/shard_map/ppermute | solution.py:939
  223.1 25.5 %collective-permute-start.23 = (bf16[192,1920]{1,0:T(8,128)(2,1)}, bf16[192,1920]{1,0:T(8,128)(2,1)S(1)}, u32[]{:S(2)}, u32[]{:S(2)}) collective-permute-start(bf16[192,1920]{1,0:T(8,128)(2,1)} %get-tuple-element.226), channel_id=1, source_target_pairs={{0,2},{1,9},{2,0},{3,11},{4,6},{5,13},{6,4},{7,15},{8,10},{9,1},{1... | collective-permute-start | bytes 2211848 | tf_op jit(solution)/shard_map/ppermute | solution.py:970
  238.8 16.7 %collective-permute-start.21 = (bf16[48,1536]{1,0:T(8,128)(2,1)}, bf16[48,1536]{1,0:T(8,128)(2,1)S(1)}, u32[]{:S(2)}, u32[]{:S(2)}) collective-permute-start(bf16[48,1536]{1,0:T(8,128)(2,1)} %get-tuple-element.260), channel_id=1, source_target_pairs={{0,16},{1,17},{2,18},{3,19},{4,20},{5,21},{6,22},{7,23},{8,24},{9,... | collective-permute-start | bytes 442376 | tf_op jit(solution)/shard_map/ppermute | solution.py:970
  243.9 23.7 %collective-permute-start.27 = (bf16[384,1152]{1,0:T(8,128)(2,1)}, bf16[384,1152]{1,0:T(8,128)(2,1)}, u32[]{:S(2)}, u32[]{:S(2)}) collective-permute-start(bf16[384,1152]{1,0:T(8,128)(2,1)} %input_weights.6), channel_id=1, source_target_pairs={{0,1},{1,0},{2,3},{3,2},{4,5},{5,4},{6,7},{7,6},{8,9},{9,8},{10,11... | collective-permute-start | bytes 2654216 | tf_op jit(solution)/shard_map/ppermute | solution.py:939
  249.7 21.6 %collective-permute-start.26 = (bf16[96,1920]{1,0:T(8,128)(2,1)}, bf16[96,1920]{1,0:T(8,128)(2,1)}, u32[]{:S(2)}, u32[]{:S(2)}) collective-permute-start(bf16[96,1920]{1,0:T(8,128)(2,1)} %get-tuple-element.250), channel_id=1, source_target_pairs={{0,8},{1,3},{2,10},{3,1},{4,12},{5,7},{6,14},{7,5},{8,0},{9,11},{1... | collective-permute-start | bytes 1105928 | tf_op jit(solution)/shard_map/ppermute | solution.py:970
  252.7 21.9 %collective-permute-start.25 = (bf16[96,768]{1,0:T(8,128)(2,1)S(1)}, bf16[96,768]{1,0:T(8,128)(2,1)S(1)}, u32[]{:S(2)}, u32[]{:S(2)}) collective-permute-start(bf16[96,768]{1,0:T(8,128)(2,1)S(1)} %get-tuple-element.218), channel_id=1, source_target_pairs={{0,16},{1,17},{2,18},{3,19},{4,20},{5,21},{6,22},{7,23},{8,24},{9,... | collective-permute-start | bytes 442376 | tf_op jit(solution)/shard_map/ppermute | solution.py:970
  256.2 19.6 %collective-permute-start.24 = (bf16[48,1536]{1,0:T(8,128)(2,1)S(1)}, bf16[48,1536]{1,0:T(8,128)(2,1)S(1)}, u32[]{:S(2)}, u32[]{:S(2)}) collective-permute-start(bf16[48,1536]{1,0:T(8,128)(2,1)S(1)} %get-tuple-element.220), channel_id=1, source_target_pairs={{0,16},{1,17},{2,18},{3,19},{4,20},{5,21},{6,22},{7,23},{8,24},{9,... | collective-permute-start | bytes 442376 | tf_op jit(solution)/shard_map/ppermute | solution.py:970
  267.5 23.2 %collective-permute-start.31 = (f32[13,768]{1,0:T(8,128)S(1)}, f32[13,768]{1,0:T(8,128)S(1)}, u32[]{:S(2)}, u32[]{:S(2)}) collective-permute-start(f32[13,768]{1,0:T(8,128)S(1)} %concatenate.100), channel_id=1, source_target_pairs={{0,1},{1,0},{2,3},{3,2},{4,5},{5,4},{6,7},{7,6},{8,9},{9,8},{10,11... | collective-permute-start | bytes 119816 | tf_op jit(solution)/shard_map/ppermute | solution.py:939
  289.5 21.2 %collective-permute-start.37 = (bf16[192,1536]{1,0:T(8,128)(2,1)S(1)}, bf16[192,1536]{1,0:T(8,128)(2,1)S(1)}, u32[]{:S(2)}, u32[]{:S(2)}) collective-permute-start(bf16[192,1536]{1,0:T(8,128)(2,1)S(1)} %pad_maximum_fusion.8), channel_id=1, source_target_pairs={{0,2},{1,9},{2,0},{3,11},{4,6},{5,13},{6,4},{7,15},{8,10},{9,1},{1... | collective-permute-start | bytes 1769480 | tf_op jit(solution)/shard_map/ppermute | solution.py:970
  298.6 32.4 %collective-permute-start.43 = (bf16[768,768]{1,0:T(8,128)(2,1)S(1)}, bf16[768,768]{1,0:T(8,128)(2,1)S(1)}, u32[]{:S(2)}, u32[]{:S(2)}) collective-permute-start(bf16[768,768]{1,0:T(8,128)(2,1)S(1)} %pad_maximum_fusion.4), channel_id=1, source_target_pairs={{0,4},{1,3},{2,6},{3,1},{4,0},{5,7},{6,2},{7,5},{8,12},{9,11},{10,... | collective-permute-start | bytes 3538952 | tf_op jit(solution)/shard_map/ppermute | solution.py:970
  301.8 27.6 %collective-permute-start.45 = (bf16[48,1152]{1,0:T(8,128)(2,1)S(1)}, bf16[48,1152]{1,0:T(8,128)(2,1)S(1)}, u32[]{:S(2)}, u32[]{:S(2)}) collective-permute-start(bf16[48,1152]{1,0:T(8,128)(2,1)S(1)} %get-tuple-element.264), channel_id=1, source_target_pairs={{0,4},{1,5},{2,6},{3,7},{4,0},{5,1},{6,2},{7,3},{8,12},{9,13},{10,... | collective-permute-start | bytes 331784 | tf_op jit(solution)/shard_map/ppermute | solution.py:970
  302.9 26.6 %collective-permute-start.44 = (bf16[24,1920]{1,0:T(8,128)(2,1)S(1)}, bf16[24,1920]{1,0:T(8,128)(2,1)S(1)}, u32[]{:S(2)}, u32[]{:S(2)}) collective-permute-start(bf16[24,1920]{1,0:T(8,128)(2,1)S(1)} %get-tuple-element.216), channel_id=1, source_target_pairs={{0,16},{1,17},{2,18},{3,19},{4,20},{5,21},{6,22},{7,23},{8,24},{9,... | collective-permute-start | bytes 276488 | tf_op jit(solution)/shard_map/ppermute | solution.py:970
  310.8 26.1 %collective-permute-start.42 = (bf16[384,1536]{1,0:T(8,128)(2,1)S(1)}, bf16[384,1536]{1,0:T(8,128)(2,1)S(1)}, u32[]{:S(2)}, u32[]{:S(2)}) collective-permute-start(bf16[384,1536]{1,0:T(8,128)(2,1)S(1)} %pad_maximum_fusion.5), channel_id=1, source_target_pairs={{0,8},{1,5},{2,10},{3,7},{4,12},{5,1},{6,14},{7,3},{8,0},{9,13},{1... | collective-permute-start | bytes 3538952 | tf_op jit(solution)/shard_map/ppermute | solution.py:970
  332.1 34.6 %collective-permute-start.52 = (bf16[1536,768]{1,0:T(8,128)(2,1)}, bf16[1536,768]{1,0:T(8,128)(2,1)}, u32[]{:S(2)}, u32[]{:S(2)}) collective-permute-start(bf16[1536,768]{1,0:T(8,128)(2,1)} %constant_dynamic-update-slice_fusion.refs_0_), channel_id=1, source_target_pairs={{0,1},{1,0},{2,3},{3,2},{4,5},{5,4},{6,7},{7,6},{8,9},{9,8},{10,11... | collective-permute-start | bytes 7077896 | tf_op jit(solution)/shard_map/ppermute | solution.py:939
  334.4 19.6 %collective-permute-start.11 = (bf16[288,768]{1,0:T(8,128)(2,1)}, bf16[288,768]{1,0:T(8,128)(2,1)S(1)}, u32[]{:S(2)}, u32[]{:S(2)}) collective-permute-start(bf16[288,768]{1,0:T(8,128)(2,1)} %get-tuple-element.126), channel_id=1, source_target_pairs={{0,3},{1,2},{2,1},{3,0},{4,7},{5,6},{6,5},{7,4},{8,11},{9,10},{10,... | collective-permute-start | bytes 1327112 | tf_op jit(solution)/shard_map/ppermute | solution.py:939
  337.9 48.0 %collective-permute-start.55 = (bf16[768,1536]{1,0:T(8,128)(2,1)}, bf16[768,1536]{1,0:T(8,128)(2,1)}, u32[]{:S(2)}, u32[]{:S(2)}) collective-permute-start(bf16[768,1536]{1,0:T(8,128)(2,1)} %constant_dynamic-update-slice_fusion.5.refs_0_), channel_id=1, source_target_pairs={{0,1},{1,0},{2,3},{3,2},{4,5},{5,4},{6,7},{7,6},{8,9},{9,8},{10,11... | collective-permute-start | bytes 7077896 | tf_op jit(solution)/shard_map/ppermute | solution.py:939
  339.9 17.6 %collective-permute-start.41 = (f32[13,768]{1,0:T(8,128)S(1)}, f32[13,768]{1,0:T(8,128)S(1)}, u32[]{:S(2)}, u32[]{:S(2)}) collective-permute-start(f32[13,768]{1,0:T(8,128)S(1)} %add.506), channel_id=1, source_target_pairs={{0,4},{4,0},{8,12},{12,8},{16,20},{20,16},{24,28},{28,24},{1,5},{5... | collective-permute-start | bytes 119816 | tf_op jit(solution)/shard_map/ppermute | solution.py:939
  365.8 55.9 %collective-permute-start.28 = (bf16[288,768]{1,0:T(8,128)(2,1)}, bf16[288,768]{1,0:T(8,128)(2,1)}, u32[]{:S(2)}, u32[]{:S(2)}) collective-permute-start(bf16[288,768]{1,0:T(8,128)(2,1)} %get-tuple-element.166), channel_id=1, source_target_pairs={{0,1},{1,0},{2,3},{3,2},{4,5},{5,4},{6,7},{7,6},{8,9},{9,8},{10,11... | collective-permute-start | bytes 1327112 | tf_op jit(solution)/shard_map/ppermute | solution.py:939
  378.1 21.9 %collective-permute-start.53 = (bf16[192,1920]{1,0:T(8,128)(2,1)}, bf16[192,1920]{1,0:T(8,128)(2,1)}, u32[]{:S(2)}, u32[]{:S(2)}) collective-permute-start(bf16[192,1920]{1,0:T(8,128)(2,1)} %pad_maximum_fusion.6), channel_id=1, source_target_pairs={{0,2},{1,9},{2,0},{3,11},{4,6},{5,13},{6,4},{7,15},{8,10},{9,1},{1... | collective-permute-start | bytes 2211848 | tf_op jit(solution)/shard_map/ppermute | solution.py:970
  379.7 18.3 %collective-permute-start.54 = (bf16[48,1152]{1,0:T(8,128)(2,1)}, bf16[48,1152]{1,0:T(8,128)(2,1)S(1)}, u32[]{:S(2)}, u32[]{:S(2)}) collective-permute-start(bf16[48,1152]{1,0:T(8,128)(2,1)} %pad_maximum_fusion.15), channel_id=1, source_target_pairs={{0,4},{1,5},{2,6},{3,7},{4,0},{5,1},{6,2},{7,3},{8,12},{9,13},{10,... | collective-permute-start | bytes 331784 | tf_op jit(solution)/shard_map/ppermute | solution.py:970
  384.7 37.0 %collective-permute-start.29 = (bf16[288,768]{1,0:T(8,128)(2,1)}, bf16[288,768]{1,0:T(8,128)(2,1)}, u32[]{:S(2)}, u32[]{:S(2)}) collective-permute-start(bf16[288,768]{1,0:T(8,128)(2,1)} %get-tuple-element.167), channel_id=1, source_target_pairs={{0,2},{1,3},{2,0},{3,1},{4,6},{5,7},{6,4},{7,5},{8,10},{9,11},{10,... | collective-permute-start | bytes 1327112 | tf_op jit(solution)/shard_map/ppermute | solution.py:939
  385.9 35.8 %collective-permute-start.30 = (bf16[288,768]{1,0:T(8,128)(2,1)}, bf16[288,768]{1,0:T(8,128)(2,1)}, u32[]{:S(2)}, u32[]{:S(2)}) collective-permute-start(bf16[288,768]{1,0:T(8,128)(2,1)} %get-tuple-element.168), channel_id=1, source_target_pairs={{0,3},{1,2},{2,1},{3,0},{4,7},{5,6},{6,5},{7,4},{8,11},{9,10},{10,... | collective-permute-start | bytes 1327112 | tf_op jit(solution)/shard_map/ppermute | solution.py:939
  407.7 20.6 %collective-permute-start.58 = (bf16[384,1920]{1,0:T(8,128)(2,1)}, bf16[384,1920]{1,0:T(8,128)(2,1)}, u32[]{:S(2)}, u32[]{:S(2)}) collective-permute-start(bf16[384,1920]{1,0:T(8,128)(2,1)} %constant_dynamic-update-slice_fusion.10.refs_0_), channel_id=1, source_target_pairs={{0,1},{1,0},{2,3},{3,2},{4,5},{5,4},{6,7},{7,6},{8,9},{9,8},{10,11... | collective-permute-start | bytes 4423688 | tf_op jit(solution)/shard_map/ppermute | solution.py:939
  (64 other events, 632.2 us)
